TPU v7x, 32 devices: a whole 2x2x4 slice. The times are simulated.
32 devices in a mesh: dp: 8 (over z, y), tensor: 4 (over x, core).
Axes of the slice: x: 2, y: 2, z: 4, core: 2. Of those that a mesh axis runs over, the one named last changes fastest.
Arguments:
- tokens_in: bfloat16 [16384, 768], P(('dp', 'tensor')), may hold values from -6 to 6
- carried_logits: float32 [16384, 12], P(('dp', 'tensor')), may hold values from -3 to 3
- cotangent: bfloat16 [16384, 768], P(('dp', 'tensor')), may hold values from -6 to 6
- segment_ids: int32 [16384], P('dp'), may hold values from 0 to 12, as said below
- parent_ids: int32 [16384], P('dp'), may hold values from 0 to 4, as said below
- routes: int32 [16384, 2], P('dp'), may hold values from 0 to 11, all different within a row; in each aligned block of 2048 rows (0 to 2047, 2048 to 4095, ...) at most 512 rows name the same one
- attention_gain: float32 [768], replicated, may hold values from 0.5 to 1.5
- head_weight: float32 [3, 768, 768], P(None, 'dp', 'tensor'), may hold values from -0.21875 to 0.21875
- output_weight: float32 [768, 768], P('tensor', 'dp'), may hold values from -2.5 to 2.5
- expert_gain: float32 [768], replicated, may hold values from 0.5 to 1.5
- router_weight: float32 [768, 12], replicated, may hold values from -0.15625 to 0.15625
- carry_weight: float32 [12, 12], replicated, may hold values from -1.25 to 1.25
- constant_gate: float32 [768, 4], replicated, may hold values from -0.21875 to 0.21875
- constant_vector: float32 [2, 768], replicated, may hold values from -6 to 6
- expert_first: float32 [8, 2, 768, 2048], P(None, None, 'dp', 'tensor'), may hold values from -0.21875 to 0.21875
- expert_second: float32 [8, 2048, 768], P(None, 'tensor', 'dp'), may hold values from -0.25 to 0.25
Outputs:
- output: bfloat16 [16384, 768], P(('dp', 'tensor'))
- grad_tokens: float32 [16384, 768], P(('dp', 'tensor'))
- grad_carried: float32 [16384, 12], P(('dp', 'tensor'))
- grad_attention_gain: float32 [768], replicated
- grad_head_weight: float32 [3, 768, 768], P(None, 'dp', 'tensor')
- grad_output_weight: float32 [768, 768], P('tensor', 'dp')
- grad_expert_gain: float32 [768], replicated
- grad_router_weight: float32 [768, 12], replicated
- grad_carry_weight: float32 [12, 12], replicated
- grad_constant_gate: float32 [768, 4], replicated
- grad_constant_vector: float32 [2, 768], replicated
- grad_expert_first: float32 [8, 2, 768, 2048], P(None, None, 'dp', 'tensor')
- grad_expert_second: float32 [8, 2048, 768], P(None, 'tensor', 'dp')
Inputs may be any that keep to these rules, and one draw needn't show every extreme that they name: `segment_ids`: in each tree (aligned blocks of 2048 tokens) the segments come in order: 0 is the trunk (the first 768 tokens), 1 to 4 are branches, the rest leaves; every segment holds a token. `parent_ids`: the parent of the trunk and of every branch is 0; each branch is the parent of two leaves. `routes`: A token's two experts differ; in each tree no expert is named by more than 512 tokens, a bound that some block reaches.
All inputs are finite; a program needn't handle non-finite values.
Results may differ from a plain program's by a relative error of at most 0.017.
Values may be sent and summed in bfloat16 or wider, within the bound.
A program may use at most 256 MiB of HBM per device.

v0:
```python
import functools

import jax
import jax.numpy as jnp
from jax import lax
from jax.experimental import pallas as pl
from jax.experimental.pallas import tpu as pltpu
from jax.sharding import PartitionSpec as P

HEAD = 64
NF = 8
NSEG = 13
NE = 12
PAD = 256
BLOCK = 256
SLICES = 4
MIX = 12
WINDOW = 1280
TILE = 256
GROUPS = 2

epsilon = 1e-06
HIGHEST = lax.Precision.HIGHEST
F32 = jnp.float32
BF16 = jnp.bfloat16
MESH = pl.DeviceIdType.MESH


def dot_nn(a, b):
    return lax.dot_general(a, b, (((1,), (0,)), ((), ())), preferred_element_type=F32)


def dot_nt(a, b):
    return lax.dot_general(a, b, (((1,), (1,)), ((), ())), preferred_element_type=F32)


def dot_tn(a, b):
    return lax.dot_general(a, b, (((0,), (0,)), ((), ())), preferred_element_type=F32)


def normed(values, gain_vector):
    return (
        values
        * lax.rsqrt(jnp.mean(values * values, axis=-1, keepdims=True) + epsilon)
        * gain_vector
    )


def tree_positions(segment, parent):
    token_count = segment.shape[0]
    labels = jnp.arange(NSEG, dtype=jnp.int32)
    own_hot = (segment[:, None] == labels[None, :]).astype(jnp.int32)
    parent_hot = (parent[:, None] == labels[None, :]).astype(jnp.int32)
    lengths = jnp.sum(own_hot, axis=0)
    starts = jnp.cumsum(lengths) - lengths
    own_start = jnp.sum(own_hot * starts[None, :], axis=1)
    parent_length = jnp.sum(parent_hot * lengths[None, :], axis=1)
    position_index = jnp.arange(token_count, dtype=jnp.int32)
    return (
        position_index
        - own_start
        + jnp.where(segment > 0, lengths[0], 0)
        + jnp.where(parent > 0, parent_length, 0)
    )


def rotary_angles(segment, parent):
    angle_rate = 10000.0 ** (-2.0 * jnp.arange(HEAD // 2, dtype=F32) / HEAD)
    angles = tree_positions(segment, parent).astype(F32)[:, None] * angle_rate[None, :]
    return jnp.concatenate([jnp.cos(angles), jnp.sin(angles)], axis=1)


def swap(values, axis, bits):
    size = lax.axis_size(axis)
    return lax.ppermute(values, axis, [(i, i ^ bits) for i in range(size)])


def together(*values):
    return lax.optimization_barrier(values)


def column_groups():
    size = lax.axis_size("dp")
    return [list(range(first, size, 2)) for first in range(2)]


def gather_column(own):
    return lax.all_gather(own, "dp", axis=0, tiled=False, axis_index_groups=column_groups())


def scatter_column(parts):
    return lax.psum_scatter(
        parts, "dp", scatter_dimension=0, tiled=False, axis_index_groups=column_groups()
    )


def by_parity(mine, other):
    even = lax.axis_index("dp") % 2 == 0
    return jnp.stack([jnp.where(even, mine, other), jnp.where(even, other, mine)])


def swap_halves(values):
    lane = lax.broadcasted_iota(jnp.int32, values.shape, 1)
    half = HEAD // 2
    return jnp.where(
        lane % HEAD < half, pltpu.roll(values, PAD - half, 1), pltpu.roll(values, half, 1)
    )


def rotation(angles):
    half = HEAD // 2
    source = lax.broadcasted_iota(jnp.int32, (2 * half, PAD), 0)
    lane = lax.broadcasted_iota(jnp.int32, (2 * half, PAD), 1)
    to_cos = (source == lane % half).astype(F32)
    to_sin = jnp.where(
        source == half + lane % half, jnp.where(lane % HEAD < half, -1.0, 1.0), 0.0
    )
    return [
        lax.dot_general(
            angles, where, (((1,), (0,)), ((), ())), precision=HIGHEST, preferred_element_type=F32
        )
        for where in (to_cos, to_sin)
    ]


def project_kernel(columns, tok_ref, gain_ref, angle_ref, pack_ref, *refs):
    q_ref, k_ref, v_ref, kt_ref, vt_ref, one_ref = refs[:6]
    if columns:
        head_ref, gathered, shards, send_sems, recv_sems = refs[6:]
    else:
        head_ref, (gathered, send_sems, recv_sems) = pack_ref, refs[6:]
    near, far, across, *column = enter(columns)
    copies = Copies(send_sems, recv_sems)
    dp, tensor = lax.axis_index("dp"), lax.axis_index("tensor")
    rows, width = tok_ref.shape
    share = pack_ref.shape[0]
    heads, last = [], []
    if columns:
        heads = [copies.start(pack_ref, shards.at[dp], device) for device in column]
        last.append(copies.start(pack_ref, shards.at[dp], across))
        shards[dp] = pack_ref[...]
    size = rows // SLICES
    slices = [pl.ds(c * size, size) for c in range(SLICES)]
    far_moves, near_moves = [], []
    for at in slices:
        values = tok_ref[at, :].astype(F32)
        scale = lax.rsqrt(jnp.mean(values * values, axis=1, keepdims=True) + epsilon)
        gathered[0, at, :] = (values * scale * gain_ref[...]).astype(BF16)
        far_moves.append(copies.start(gathered.at[0, at], gathered.at[2, at], far))
        near_moves.append(copies.start(gathered.at[0, at], gathered.at[1, at], near))
    corner_moves = []
    for c, at in enumerate(slices):
        far_moves[c].wait_recv()
        corner_moves.append(copies.start(gathered.at[2, at], gathered.at[3, at], near))
        if c < len(heads):
            heads[c].wait_recv()
            origin = lax.rem(dp + 8 - 2 * (c + 1), 8)
            last.append(copies.start(shards.at[origin], shards.at[origin], across))
    for move in last + near_moves + corner_moves:
        move.wait_recv()
    if columns:
        for d in range(8):
            at = pl.ds(d * share, share)
            piece = shards[d]
            for section in range(4):
                head_ref[at, section * PAD : section * PAD + 128] = piece[
                    :, section * 128 : (section + 1) * 128
                ]
                start = 512 + 128 * (section // 2)
                rest = piece[:, start : start + 128].astype(F32)
                if section % 2:
                    rest = pltpu.roll(rest, 64, 1)
                lane = lax.broadcasted_iota(jnp.int32, rest.shape, 1)
                head_ref[at, section * PAD + 128 : (section + 1) * PAD] = jnp.where(
                    lane < 64, rest, 0.0
                ).astype(BF16)
    for bits in range(4):
        start = pl.multiple_of(other(tensor, bits) * rows, rows)
        at = pl.ds(start, rows)
        values = gathered[bits]
        one_ref[at, :] = values
        cosine, sine = rotation(angle_ref[at, :])
        part = dot_nn(values, head_ref[:, :PAD])
        q_ref[at, :] = ((part * cosine + swap_halves(part) * sine) * HEAD**-0.5).astype(BF16)
        part = dot_nn(values, head_ref[:, PAD : 2 * PAD])
        part = part * cosine + swap_halves(part) * sine
        k_ref[at, :] = part.astype(BF16)
        kt_ref[:, at] = part.T.astype(BF16)
        part = dot_nn(values, head_ref[:, 2 * PAD : 3 * PAD])
        v_ref[at, :] = part.astype(BF16)
        vt_ref[:, at] = part.T.astype(BF16)
    copies.finish()


def project(columns, tokens, gain, angles, pack):
    rows, width = tokens.shape
    total = angles.shape[0]
    vmem = pl.BlockSpec(memory_space=pltpu.VMEM)
    copies = 3 * SLICES + 7
    wide = jax.ShapeDtypeStruct((total, PAD), BF16)
    tall = jax.ShapeDtypeStruct((PAD, total), BF16)
    shapes = [wide, wide, wide, tall, tall, jax.ShapeDtypeStruct((total, width), BF16)]
    scratch = [pltpu.VMEM((4, rows, width), BF16)]
    if columns:
        shapes.append(jax.ShapeDtypeStruct((width, 4 * PAD), BF16))
        scratch.append(pltpu.VMEM((8, *pack.shape), BF16))
    out = pl.pallas_call(
        functools.partial(project_kernel, columns),
        in_specs=[vmem] * 4,
        out_specs=[vmem] * len(shapes),
        out_shape=shapes,
        scratch_shapes=scratch
        + [pltpu.SemaphoreType.DMA((copies,)), pltpu.SemaphoreType.DMA((copies,))],
        compiler_params=pltpu.CompilerParams(
            collective_id=3, has_side_effects=True, vmem_limit_bytes=56 << 20
        ),
        cost_estimate=pl.CostEstimate(
            flops=6 * total * width * PAD, bytes_accessed=16 * total * width, transcendentals=0
        ),
    )(tokens, gain[None], angles, pack)
    return out if columns else [*out, pack]


def head_mask(values, head):
    lane = lax.broadcasted_iota(jnp.int32, values.shape, 1)
    return jnp.where(lane // HEAD == head, values, jnp.zeros_like(values))


def seen(i, j, seg_row, par_row, seg_col):
    key_at = j * BLOCK + lax.broadcasted_iota(jnp.int32, (BLOCK, 1), 0)
    query_at = i * BLOCK + lax.broadcasted_iota(jnp.int32, (1, BLOCK), 1)
    related = (seg_col == seg_row) | (seg_col == par_row) | (seg_col == 0)
    return related & (key_at <= query_at)


def attend_block(heads, i, q_ref, k_ref, vt_ref, rowinfo_ref, colinfo_ref, o_ref, total_ref):
    here = pl.ds(pl.multiple_of(i * BLOCK, BLOCK), BLOCK)
    queries = q_ref[here, :]
    by_head = [head_mask(queries, h) for h in range(heads)]
    seg_row, par_row = rowinfo_ref[0:1, here], rowinfo_ref[1:2, here]

    def step(j, carry):
        at = pl.ds(pl.multiple_of(j * BLOCK, BLOCK), BLOCK)
        keys = k_ref[at, :]
        visible = seen(i, j, seg_row, par_row, colinfo_ref[at, 0:1])
        out = []
        for h in range(heads):
            top, total, mixed = carry[h]
            scores = jnp.where(visible, dot_nt(keys, by_head[h]), -1e30)
            new_top = jnp.maximum(top, jnp.max(scores, axis=0, keepdims=True))
            shrink = jnp.exp(top - new_top)
            probs = jnp.exp(scores - new_top)
            total = total * shrink + jnp.sum(probs, axis=0, keepdims=True)
            mixed = mixed * shrink + dot_nn(
                vt_ref[h * HEAD : (h + 1) * HEAD, at], probs.astype(BF16)
            )
            out.append((new_top, total, mixed))
        return tuple(out)

    start = tuple(
        (
            jnp.full((1, BLOCK), -1e30, F32),
            jnp.zeros((1, BLOCK), F32),
            jnp.zeros((HEAD, BLOCK), F32),
        )
        for _ in range(heads)
    )
    done = lax.fori_loop(0, i + 1, step, start)
    mixed = [m / t for _, t, m in done] + [jnp.zeros((PAD - heads * HEAD, BLOCK), F32)]
    o_ref[here, :] = jnp.concatenate(mixed, axis=0).T.astype(BF16)
    total_ref[:, here] = jnp.concatenate(
        [m + jnp.log(t) for m, t, _ in done] + [jnp.zeros((8 - heads, BLOCK), F32)], axis=0
    )


def other(place, bits):
    if bits & 2:
        place = place + 2 - 4 * lax.rem(lax.div(place, 2), 2)
    if bits & 1:
        place = place + 1 - 2 * lax.rem(place, 2)
    return place


def enter(columns=False):
    dp, tensor = lax.axis_index("dp"), lax.axis_index("tensor")
    others = [(dp, other(tensor, 1)), (dp, other(tensor, 2)), (other(dp, 1), tensor)]
    if columns:
        others += [(lax.rem(dp + 2 * j, 8), tensor) for j in (1, 2, 3)]
    barrier = pltpu.get_barrier_semaphore()
    for device in others:
        pl.semaphore_signal(barrier, inc=1, device_id=device, device_id_type=MESH)
    pl.semaphore_wait(barrier, len(others))
    return others


class Copies:
    def __init__(self, send_sems, recv_sems):
        self.send_sems, self.recv_sems, self.made = send_sems, recv_sems, []

    def start(self, source, target, device):
        k = len(self.made)
        copy = pltpu.make_async_remote_copy(
            src_ref=source,
            dst_ref=target,
            send_sem=self.send_sems.at[k],
            recv_sem=self.recv_sems.at[k],
            device_id=device,
            device_id_type=MESH,
        )
        copy.start()
        self.made.append(copy)
        return copy

    def finish(self):
        for copy in self.made:
            copy.wait_send()


def quarter(ref, bits, rows):
    place = other(lax.axis_index("tensor"), bits)
    return ref.at[pl.ds(pl.multiple_of(place * rows, rows), rows)]


def sum_of_quarters(part, copies, near, far, near_send, near_recv, far_send, far_recv):
    rows = far_send.shape[0]
    near_send[0] = part(3).astype(BF16)
    first = copies.start(near_send.at[0], near_recv.at[0], near)
    near_send[1] = part(1).astype(BF16)
    second = copies.start(near_send.at[1], near_recv.at[1], near)
    mine = part(2)
    first.wait_recv()
    far_send[...] = (mine + near_recv[0].astype(F32)).astype(BF16)
    moves = []
    for c in range(SLICES):
        at = pl.ds(c * rows // SLICES, rows // SLICES)
        moves.append(copies.start(far_send.at[at], far_recv.at[at], far))
    mine = part(0)
    second.wait_recv()
    return mine + near_recv[1].astype(F32), moves


class Spread:
    def __init__(self, copies, devices, target, rows):
        self.copies, (self.near, self.far, self.across) = copies, devices
        self.rows, self.own, self.beside = rows, quarter(target.at[0], 0, rows), quarter(target.at[1], 0, rows)
        self.over, self.corner = quarter(target.at[0], 2, rows), quarter(target.at[1], 2, rows)
        self.from_far, self.from_across, self.from_corner, self.ends = {}, {}, {}, []

    def send(self, source, at, c):
        copies = self.copies
        self.from_far[c] = copies.start(source.at[at], self.own.at[at], self.far)
        self.from_across[c] = copies.start(source.at[at], self.beside.at[at], self.across)
        self.ends.append(copies.start(source.at[at], self.own.at[at], self.near))

    def pass_on(self, c, at):
        copies = self.copies
        self.from_far[c].wait_recv()
        if c >= SLICES // 2:
            self.from_corner[c] = copies.start(self.over.at[at], self.corner.at[at], self.across)
        self.ends.append(copies.start(self.over.at[at], self.over.at[at], self.near))
        self.from_across[c].wait_recv()
        if c < SLICES // 2:
            self.from_corner[c] = copies.start(self.beside.at[at], self.beside.at[at], self.far)
        self.ends.append(copies.start(self.beside.at[at], self.beside.at[at], self.near))

    def pass_corner(self, c, at):
        self.from_corner[c].wait_recv()
        self.ends.append(self.copies.start(self.corner.at[at], self.corner.at[at], self.near))

    def finish(self):
        for copy in self.ends:
            copy.wait_recv()


def branch_kernel(
    heads, q_ref, k_ref, vt_ref, rowinfo_ref, colinfo_ref, cot_ref,
    out_ref, tok_ref, gain_ref, carried_ref, mix_ref, picked_ref,
    att_ref, total_ref, hidden_ref, aux_ref, rows_ref, cots_ref,
    near_send, near_recv, far_send, far_recv, own, send_sems, recv_sems, local_sems,
):
    devices = enter()
    near, far, _ = devices
    copies = Copies(send_sems, recv_sems)
    rows, width = tok_ref.shape
    weights = out_ref[...]
    size = rows // SLICES
    slices = [pl.ds(c * size, size) for c in range(SLICES)]
    locals_ = [pltpu.make_async_copy(cot_ref, quarter(cots_ref.at[0], 0, rows), local_sems.at[0])]
    locals_[0].start()
    cots = Spread(copies, devices, cots_ref, rows)
    for c, at in enumerate(slices):
        cots.send(cot_ref, at, c)

    def part(bits):
        if bits == 0:
            for c, at in enumerate(slices):
                cots.pass_on(c, at)
        place = other(lax.axis_index("tensor"), bits)
        for block in range(rows // BLOCK):
            attend_block(
                heads, place * (rows // BLOCK) + block,
                q_ref, k_ref, vt_ref, rowinfo_ref, colinfo_ref, att_ref, total_ref,
            )
        return dot_nt(quarter(att_ref, bits, rows)[...], weights)

    mine, moves = sum_of_quarters(
        part, copies, near, far, near_send, near_recv, far_send, far_recv
    )
    hidden_ref[...] = tok_ref[...].astype(F32) + mine
    spread = Spread(copies, devices, rows_ref, rows)
    for c, at in enumerate(slices):
        moves[c].wait_recv()
        hidden = hidden_ref[at, :] + far_recv[at, :].astype(F32)
        hidden_ref[at, :] = hidden
        scale = lax.rsqrt(jnp.mean(hidden * hidden, axis=1, keepdims=True) + epsilon)
        normed_two = hidden * scale * gain_ref[...]
        logits = carried_ref[at, :] + lax.dot_general(
            normed_two,
            mix_ref[...],
            (((1,), (0,)), ((), ())),
            precision=HIGHEST,
            preferred_element_type=F32,
        )
        picked = picked_ref[at, :] > 0
        top = jnp.max(jnp.where(picked, logits, -1e30), axis=1, keepdims=True)
        weight = jnp.where(picked, jnp.exp(jnp.where(picked, logits - top, 0.0)), 0.0)
        gate = weight / jnp.sum(weight, axis=1, keepdims=True)
        lane = lax.broadcasted_iota(jnp.int32, logits.shape, 1)
        turned = jnp.where(
            lane % 2 == 0, pltpu.roll(logits, 127, 1), pltpu.roll(logits, 1, 1)
        )
        top = jnp.maximum(logits, turned)
        mixture = jnp.exp(logits - top) / (jnp.exp(logits - top) + jnp.exp(turned - top))
        aux_ref[at, :] = jnp.where(lane < MIX, gate, jnp.where(lane < MIX + 4, mixture, 0.0))
        own[at, :width] = normed_two.astype(BF16)
        own[at, width:] = jnp.where(lane < NF, gate, 0.0).astype(BF16)
        spread.send(own, at, c)
        local = pltpu.make_async_copy(
            own.at[at], quarter(rows_ref.at[0], 0, rows).at[at], local_sems.at[1 + c]
        )
        local.start()
        locals_.append(local)
    for c, at in enumerate(slices):
        cots.pass_corner(c, at)
    for c, at in enumerate(slices):
        spread.pass_on(c, at)
    for c, at in enumerate(slices):
        spread.pass_corner(c, at)
    cots.finish()
    spread.finish()
    for local in locals_:
        local.wait()
    copies.finish()


def branch(
    heads, queries, keys, values_t, rowinfo, colinfo, cotangent, head_full, tokens, gain, carried, mix,
    picked,
):
    rows, width = tokens.shape
    total = queries.shape[0]
    vmem, anywhere = pl.BlockSpec(memory_space=pltpu.VMEM), pl.BlockSpec(memory_space=pl.ANY)
    copies = 2 + 15 * SLICES
    return pl.pallas_call(
        functools.partial(branch_kernel, heads),
        in_specs=[vmem] * 12,
        out_specs=[vmem] * 4 + [anywhere] * 2,
        out_shape=[
            jax.ShapeDtypeStruct((total, PAD), BF16),
            jax.ShapeDtypeStruct((8, total), F32),
            jax.ShapeDtypeStruct((rows, width), F32),
            jax.ShapeDtypeStruct((rows, 128), F32),
            jax.ShapeDtypeStruct((2, total, width + 128), BF16),
            jax.ShapeDtypeStruct((2, total, width), BF16),
        ],
        scratch_shapes=[
            pltpu.VMEM((2, rows, width), BF16),
            pltpu.VMEM((2, rows, width), BF16),
            pltpu.VMEM((rows, width), BF16),
            pltpu.VMEM((rows, width), BF16),
            pltpu.VMEM((rows, width + 128), BF16),
            pltpu.SemaphoreType.DMA((copies,)),
            pltpu.SemaphoreType.DMA((copies,)),
            pltpu.SemaphoreType.DMA((1 + SLICES,)),
        ],
        compiler_params=pltpu.CompilerParams(
            collective_id=1, has_side_effects=True, vmem_limit_bytes=48 << 20
        ),
        cost_estimate=pl.CostEstimate(
            flops=64 * rows * width * PAD, bytes_accessed=64 * rows * width, transcendentals=0
        ),
    )(
        queries, keys, values_t, rowinfo, colinfo, cotangent, head_full[:, 3 * PAD :], tokens, gain[None],
        carried, mix, picked,
    )


class PairSum:
    def __init__(self, copies, devices, source, refs, local_sems):
        self.copies, (self.near, self.far, self.across) = copies, devices
        self.source, self.local_sems = source, local_sems
        self.kept, self.near_recv, self.corner_send, self.corner_recv = refs[:4]
        self.far_send, self.far_recv, self.across_send, self.across_recv = refs[4:]
        self.rows = self.far_send.shape[0]
        half = self.rows // 2
        self.halves = [pl.ds(0, half), pl.ds(half, half)]
        self.arrivals, self.locals_, self.from_far, self.from_across = {}, {}, {}, {}

    @staticmethod
    def shapes(rows, wide):
        one, two = (rows, wide), (2, rows // 2, wide)
        return [
            pltpu.VMEM(shape, BF16)
            for shape in ((4, *one), (4, *one), one, two, one, one, one, one)
        ]

    def start(self):
        for b in (3, 1, 2, 0):
            tree, bits = self.source.at[b // 2], 2 * (b % 2)
            self.arrivals[b] = self.copies.start(
                quarter(tree, bits + 1, self.rows), self.near_recv.at[b], self.near
            )
            self.locals_[b] = pltpu.make_async_copy(
                quarter(tree, bits, self.rows), self.kept.at[b], self.local_sems.at[b]
            )
            self.locals_[b].start()

    def joined(self, b, at):
        return self.kept[b, at, :].astype(F32) + self.near_recv[b, at, :].astype(F32)

    def arrived(self, b):
        self.arrivals[b].wait_recv()
        self.locals_[b].wait()

    def first_round(self):
        low, high = self.halves
        self.arrived(3)
        self.corner_send[...] = self.joined(3, pl.ds(0, self.rows)).astype(BF16)
        start = self.copies.start
        self.corner_far = start(self.corner_send.at[low], self.corner_recv.at[0], self.far)
        self.corner_across = start(self.corner_send.at[high], self.corner_recv.at[1], self.across)
        self.arrived(1)
        self.far_send[low, :] = self.joined(1, low).astype(BF16)
        self.from_far[0] = start(self.far_send.at[low], self.far_recv.at[low], self.far)
        self.arrived(2)
        self.across_send[high, :] = self.joined(2, high).astype(BF16)
        self.from_across[1] = start(self.across_send.at[high], self.across_recv.at[high], self.across)

    def second_round(self):
        low, high = self.halves
        start = self.copies.start
        self.corner_far.wait_recv()
        self.across_send[low, :] = (
            self.joined(2, low) + self.corner_recv[0].astype(F32)
        ).astype(BF16)
        self.from_across[0] = start(self.across_send.at[low], self.across_recv.at[low], self.across)
        self.corner_across.wait_recv()
        self.far_send[high, :] = (
            self.joined(1, high) + self.corner_recv[1].astype(F32)
        ).astype(BF16)
        self.from_far[1] = start(self.far_send.at[high], self.far_recv.at[high], self.far)
        self.arrived(0)

    def total(self, h):
        self.from_far[h].wait_recv()
        self.from_across[h].wait_recv()
        at = self.halves[h]
        return (
            self.joined(0, at)
            + self.far_recv[at, :].astype(F32)
            + self.across_recv[at, :].astype(F32)
        )


def attend_back_block(
    heads, i, q_ref, g_ref, o_ref, k_ref, v_ref, kt_ref, rowinfo_ref, colinfo_ref, total_ref, angle_ref,
    grad_ref, key_sum, value_sum, query_sum,
):
    here = pl.ds(pl.multiple_of(i * BLOCK, BLOCK), BLOCK)
    query_sum[...] = jnp.zeros_like(query_sum)
    queries, grads = q_ref[here, :], g_ref[here, :]
    q_heads = [head_mask(queries, h) for h in range(heads)]
    g_heads = [head_mask(grads, h) for h in range(heads)]
    seg_row, par_row = rowinfo_ref[0:1, here], rowinfo_ref[1:2, here]
    product = grads.astype(F32) * o_ref[here, :].astype(F32)
    lane = lax.broadcasted_iota(jnp.int32, (8, PAD), 1)
    which = lax.broadcasted_iota(jnp.int32, (8, PAD), 0)
    delta = lax.dot_general(
        (lane // HEAD == which).astype(F32),
        product,
        (((1,), (1,)), ((), ())),
        precision=HIGHEST,
        preferred_element_type=F32,
    )
    totals = total_ref[:, here]

    def step(j, carry):
        at = pl.ds(pl.multiple_of(j * BLOCK, BLOCK), BLOCK)
        keys, values = k_ref[at, :], v_ref[at, :]
        visible = seen(i, j, seg_row, par_row, colinfo_ref[at, 0:1])
        key_part, value_part = key_sum[at, :], value_sum[at, :]
        for h in range(heads):
            scores = jnp.where(visible, dot_nt(keys, q_heads[h]), -1e30)
            probs = jnp.exp(scores - totals[h : h + 1, :])
            value_part = value_part + dot_nn(probs.astype(BF16), g_heads[h])
            grad_probs = dot_nt(values, g_heads[h])
            grad_scores = (probs * (grad_probs - delta[h : h + 1, :])).astype(BF16)
            key_part = key_part + dot_nn(grad_scores, q_heads[h])
            lanes = slice(h * HEAD, (h + 1) * HEAD)
            query_sum[lanes, :] += dot_nn(kt_ref[lanes, at], grad_scores)
        key_sum[at, :] = key_part
        value_sum[at, :] = value_part
        return carry

    lax.fori_loop(0, i + 1, step, 0)
    grad_ref[here, :PAD] = turned_back(query_sum[...].T * HEAD**-0.5, angle_ref[here, :])


def turned_back(values, angles):
    cosine, sine = rotation(angles)
    return (values * cosine - swap_halves(values) * sine).astype(BF16)


def branch_back_kernel(
    heads, hidden_ref, aux_ref, cot_ref, gain_ref, mix_ref, vector_ref, carried_ref, att_ref, out_ref,
    q_ref, k_ref, v_ref, kt_ref, rowinfo_ref, colinfo_ref, total_ref, angle_ref, sums_ref, grad_ins_ref,
    grad_hidden_ref, grad_logits_ref, grad_out_ref, small_ref, grad_ref, result_ref,
    normed_two, base, gathered, grad_att, key_sum, value_sum, query_sum,
    send_sems, recv_sems, local_sems, *buffers,
):
    devices = enter()
    near, far, _ = devices
    copies = Copies(send_sems, recv_sems)
    rows, width = hidden_ref.shape
    half = rows // 2
    halves = [pl.ds(0, half), pl.ds(half, half)]
    incoming = PairSum(copies, devices, grad_ins_ref, buffers[:8], local_sems.at[0])
    results = PairSum(copies, devices, sums_ref, buffers[8:], local_sems.at[1])
    incoming.start()
    key_sum[...] = jnp.zeros_like(key_sum)
    value_sum[...] = jnp.zeros_like(value_sum)

    gain = gain_ref[...]
    lane = lax.broadcasted_iota(jnp.int32, (half, 128), 1)

    def column(values, at):
        return jnp.sum(jnp.where(lane == at, values, 0.0), axis=1, keepdims=True)

    known = []
    for at in halves:
        hidden, aux, grads = hidden_ref[at, :], aux_ref[at, :], cot_ref[at, :].astype(F32)
        scale = lax.rsqrt(jnp.mean(hidden * hidden, axis=1, keepdims=True) + epsilon)
        normed = hidden * scale * gain
        normed_two[at, :] = normed
        gates = [column(aux, NF + 1 + k) for k in range(3)]
        mixes = [column(aux, MIX + k) for k in range(4)]
        along = jnp.sum(grads * normed, axis=1, keepdims=True)
        vectors = [
            jnp.sum(grads * vector_ref[c : c + 1, :], axis=1, keepdims=True) for c in range(2)
        ]
        kept = gates[0] + gates[1] * mixes[0] + gates[2] * mixes[2]
        base[at, :] = grads * kept
        sums = []
        for c in range(2):
            sums.append(
                jnp.sum(grads * (gates[1 + c] * mixes[2 * c + 1]), axis=0, keepdims=True)
            )
        by_gate = jnp.where(lane == NF + 1, along, 0.0)
        by_mix = jnp.zeros((half, 128), F32)
        for c in range(2):
            first, second = mixes[2 * c], mixes[2 * c + 1]
            by_gate = by_gate + jnp.where(
                lane == NF + 2 + c, first * along + second * vectors[c], 0.0
            )
            d_first, d_second = gates[1 + c] * along, gates[1 + c] * vectors[c]
            inner = first * d_first + second * d_second
            by_mix = by_mix + jnp.where(lane == MIX + 2 * c, first * (d_first - inner), 0.0)
            by_mix = by_mix + jnp.where(lane == MIX + 2 * c + 1, second * (d_second - inner), 0.0)
        known.append((scale, by_gate, by_mix, sums))
    incoming.first_round()
    incoming.second_round()

    gain_sum = jnp.zeros((1, width), F32)
    far_moves, near_moves = [], []
    for h, at in enumerate(halves):
        scale, by_gate, by_mix, _ = known[h]
        arriving = incoming.total(h)
        by_gate = by_gate + jnp.where(lane < NF, arriving[:, width:], 0.0)
        gates = jnp.where(lane < MIX, aux_ref[at, :], 0.0)
        grad_logits = by_mix + gates * (
            by_gate - jnp.sum(gates * by_gate, axis=1, keepdims=True)
        )
        grad_logits_ref[at, :] = grad_logits
        grad_normed = arriving[:, :width] + base[at, :] + lax.dot_general(
            grad_logits,
            mix_ref[...],
            (((1,), (1,)), ((), ())),
            precision=HIGHEST,
            preferred_element_type=F32,
        )
        hidden = hidden_ref[at, :]
        gain_sum = gain_sum + jnp.sum(hidden * scale * grad_normed, axis=0, keepdims=True)
        weighted = gain * grad_normed
        inner = jnp.mean(hidden * weighted, axis=1, keepdims=True)
        grad_hidden = (
            cot_ref[at, :].astype(F32) + scale * weighted - hidden * (scale * scale * scale * inner)
        )
        grad_hidden_ref[at, :] = grad_hidden
        gathered[0, at, :] = grad_hidden.astype(BF16)
        far_moves.append(copies.start(gathered.at[0, at], gathered.at[2, at], far))
        near_moves.append(copies.start(gathered.at[0, at], gathered.at[1, at], near))
    results.start()

    def over_tokens(a, b):
        return lax.dot_general(
            a, b, (((0,), (0,)), ((), ())), precision=HIGHEST, preferred_element_type=F32
        )

    small_ref[...] = jnp.zeros_like(small_ref)
    small_ref[:16, :width] = over_tokens(grad_logits_ref[...], normed_two[...])[:16]
    small_ref[16:, :width] = jnp.concatenate(
        [gain_sum] + [known[0][3][c] + known[1][3][c] for c in range(2)]
        + [jnp.zeros((5, width), F32)],
        axis=0,
    )
    small_ref[:16, width:] = over_tokens(carried_ref[...], grad_logits_ref[...])[:16]

    def attention_back(bits):
        values = gathered[bits]
        quarter(grad_att, bits, rows)[...] = dot_nn(values, out_ref[...]).astype(BF16)
        product = dot_tn(values, quarter(att_ref, bits, rows)[...])
        grad_out_ref[...] = grad_out_ref[...] + product if bits else product
        place = other(lax.axis_index("tensor"), bits)
        for block in range(rows // BLOCK):
            attend_back_block(
                heads, place * (rows // BLOCK) + block, q_ref, grad_att, att_ref, k_ref, v_ref, kt_ref,
                rowinfo_ref, colinfo_ref, total_ref, angle_ref, grad_ref, key_sum, value_sum, query_sum,
            )

    attention_back(0)
    results.first_round()
    for move in near_moves:
        move.wait_recv()
    last = []
    for h, at in enumerate(halves):
        far_moves[h].wait_recv()
        last.append(copies.start(gathered.at[2, at], gathered.at[3, at], near))
    attention_back(1)
    results.second_round()
    attention_back(2)
    for move in last:
        move.wait_recv()
    attention_back(3)
    for h, at in enumerate(halves):
        aux = aux_ref[at, :]
        gates = [column(aux, NF + 1 + k) for k in range(3)]
        mixes = [column(aux, MIX + k) for k in range(4)]
        kept = gates[0] + gates[1] * mixes[0] + gates[2] * mixes[2]
        result = hidden_ref[at, :] + kept * normed_two[at, :] + results.total(h)
        for c in range(2):
            result = result + (gates[1 + c] * mixes[2 * c + 1]) * vector_ref[c : c + 1, :]
        result_ref[at, :] = result.astype(BF16)

    def finish_keys(j, carry):
        at = pl.ds(pl.multiple_of(j * BLOCK, BLOCK), BLOCK)
        grad_ref[at, PAD : 2 * PAD] = turned_back(key_sum[at, :], angle_ref[at, :])
        grad_ref[at, 2 * PAD :] = value_sum[at, :].astype(BF16)
        return carry

    lax.fori_loop(0, grad_ref.shape[0] // BLOCK, finish_keys, 0)
    copies.finish()


def branch_back(
    heads, hidden, aux, cotangent, gain, mix, vectors, carried, attended, head_full, queries, keys, values,
    keys_t, rowinfo, colinfo, totals, angles, sums, grad_ins,
):
    rows, width = hidden.shape
    total = queries.shape[0]
    vmem, anywhere = pl.BlockSpec(memory_space=pltpu.VMEM), pl.BlockSpec(memory_space=pl.ANY)
    copies = 2 * 10 + 6
    return pl.pallas_call(
        functools.partial(branch_back_kernel, heads),
        in_specs=[vmem] * 17 + [anywhere] * 2,
        out_specs=[vmem] * 6,
        out_shape=[
            jax.ShapeDtypeStruct((rows, width), F32),
            jax.ShapeDtypeStruct((rows, 128), F32),
            jax.ShapeDtypeStruct((width, PAD), F32),
            jax.ShapeDtypeStruct((24, width + 128), F32),
            jax.ShapeDtypeStruct((total, 3 * PAD), BF16),
            jax.ShapeDtypeStruct((rows, width), BF16),
        ],
        scratch_shapes=[
            pltpu.VMEM((rows, width), F32),
            pltpu.VMEM((rows, width), F32),
            pltpu.VMEM((4, rows, width), BF16),
            pltpu.VMEM((total, PAD), BF16),
            pltpu.VMEM((total, PAD), F32),
            pltpu.VMEM((total, PAD), F32),
            pltpu.VMEM((PAD, BLOCK), F32),
            pltpu.SemaphoreType.DMA((copies,)),
            pltpu.SemaphoreType.DMA((copies,)),
            pltpu.SemaphoreType.DMA((2, 4)),
        ]
        + PairSum.shapes(rows, grad_ins.shape[2])
        + PairSum.shapes(rows, width),
        compiler_params=pltpu.CompilerParams(
            collective_id=2, has_side_effects=True, vmem_limit_bytes=61 << 20
        ),
        cost_estimate=pl.CostEstimate(
            flops=256 * rows * width * PAD, bytes_accessed=64 * rows * width, transcendentals=0
        ),
    )(
        hidden, aux, cotangent, gain[None], mix, vectors, carried, attended, head_full[:, 3 * PAD :],
        queries, keys, values, keys_t, rowinfo, colinfo, totals, angles, sums, grad_ins,
    )


def finish_kernel(
    columns, grad_ref, one_ref, head_ref, grad_out_ref, small_ref, grad_hidden_ref, tok_ref, gain_ref,
    *refs
):
    grad_tok_ref, pack_ref, sum_ref, refs = refs[0], refs[1], refs[2], refs[3:]
    near_send, near_recv, far_send, far_recv, send_sems, recv_sems = refs[:6]
    near, far, across, *column = enter(columns)
    copies = Copies(send_sems, recv_sems)
    dp = lax.axis_index("dp")
    rows, width = tok_ref.shape
    share = width // 8

    def part(bits):
        return dot_nt(quarter(grad_ref, bits, rows)[...], head_ref[:, : 3 * PAD])

    mine, moves = sum_of_quarters(
        part, copies, near, far, near_send, near_recv, far_send, far_recv
    )
    grad_tok_ref[...] = mine

    packed = refs[6] if columns else pack_ref
    along = jnp.zeros((8, width), F32)
    rest = None
    for section in range(4):
        at = slice(section * PAD, (section + 1) * PAD)
        if section < 3:
            grad = dot_tn(one_ref[...], grad_ref[:, at])
            along = along + lax.dot_general(
                jnp.ones((8, PAD), F32),
                grad * head_ref[:, at].astype(F32),
                (((1,), (1,)), ((), ())),
                precision=HIGHEST,
                preferred_element_type=F32,
            )
        else:
            grad = grad_out_ref[...]
        if not columns:
            packed[:, at] = grad.astype(BF16)
            continue
        low, high = grad[:, :128].astype(BF16), grad[:, 128:]
        if section % 2 == 0:
            rest = high
        else:
            lane = lax.broadcasted_iota(jnp.int32, high.shape, 1)
            rest = jnp.where(lane < 64, rest, pltpu.roll(high, 64, 1)).astype(BF16)
        for d in range(8):
            cut = slice(d * share, (d + 1) * share)
            packed[d, :, section * 128 : (section + 1) * 128] = low[cut]
            if section % 2:
                start = 512 + 128 * (section // 2)
                packed[d, :, start : start + 128] = rest[cut]
    small = small_ref[...]
    row = lax.broadcasted_iota(jnp.int32, (24, width), 0)
    small = jnp.concatenate(
        [
            jnp.where(row == 19, along[:1] / gain_ref[...], small[:, :width]),
            small[:, width:],
        ],
        axis=1,
    )
    if columns:
        _, pair_recv, column_send, column_recv, sums, sum_recv = refs[6:]
        pair_moves = []
        for j in range(4):
            there = lax.rem(other(dp, 1) + 2 * j, 8)
            pair_moves.append(copies.start(packed.at[there], pair_recv.at[j], across))
        sums[0] = small
        steps = [near, far, across, (other(dp, 2), lax.axis_index("tensor")), column[1]]
        sum_moves = [copies.start(sums.at[0], sum_recv.at[0], steps[0])]

        def add_up():
            k = len(sum_moves)
            sum_moves[-1].wait_recv()
            if k < 5:
                sums[k] = sums[k - 1] + sum_recv[k - 1]
                sum_moves.append(copies.start(sums.at[k], sum_recv.at[k], steps[k]))
            else:
                sum_ref[...] = sums[4] + sum_recv[4]

        add_up()
        add_up()
        column_moves = []
        for j in (1, 2, 3, 0):
            pair_moves[j].wait_recv()
            paired = packed[lax.rem(dp + 2 * j, 8)].astype(F32) + pair_recv[j].astype(F32)
            if j:
                column_send[j - 1] = paired.astype(BF16)
                column_moves.append(
                    copies.start(column_send.at[j - 1], column_recv.at[j - 1], column[j - 1])
                )
            else:
                pack_ref[...] = paired
        add_up()
    else:
        sum_ref[...] = small

    size = rows // SLICES
    for c in range(SLICES):
        at = pl.ds(c * size, size)
        moves[c].wait_recv()
        grad_normed = grad_tok_ref[at, :] + far_recv[at, :].astype(F32)
        values = tok_ref[at, :].astype(F32)
        scale = lax.rsqrt(jnp.mean(values * values, axis=1, keepdims=True) + epsilon)
        weighted = gain_ref[...] * grad_normed
        inner = jnp.mean(values * weighted, axis=1, keepdims=True)
        grad_tok_ref[at, :] = (
            grad_hidden_ref[at, :] + scale * weighted - values * (scale * scale * scale * inner)
        )
    if columns:
        add_up()
        for j in range(3):
            column_moves[j].wait_recv()
            pack_ref[...] = pack_ref[...] + column_recv[j].astype(F32)
        add_up()
    copies.finish()


def finish(columns, grads, ones, head_full, grad_out, small, grad_hidden, tokens, gain):
    rows, width = tokens.shape
    share = width // 8
    vmem = pl.BlockSpec(memory_space=pltpu.VMEM)
    copies = 2 + SLICES + 12
    pack = (
        jax.ShapeDtypeStruct((share, width), F32)
        if columns
        else jax.ShapeDtypeStruct(head_full.shape, BF16)
    )
    scratch = [
        pltpu.VMEM((2, rows, width), BF16),
        pltpu.VMEM((2, rows, width), BF16),
        pltpu.VMEM((rows, width), BF16),
        pltpu.VMEM((rows, width), BF16),
        pltpu.SemaphoreType.DMA((copies,)),
        pltpu.SemaphoreType.DMA((copies,)),
    ]
    if columns:
        scratch += [
            pltpu.VMEM((8, share, width), BF16),
            pltpu.VMEM((4, share, width), BF16),
            pltpu.VMEM((3, share, width), BF16),
            pltpu.VMEM((3, share, width), BF16),
            pltpu.VMEM((5, *small.shape), F32),
            pltpu.VMEM((5, *small.shape), F32),
        ]
    return pl.pallas_call(
        functools.partial(finish_kernel, columns),
        in_specs=[vmem] * 8,
        out_specs=[vmem] * 3,
        out_shape=[
            jax.ShapeDtypeStruct((rows, width), F32),
            pack,
            jax.ShapeDtypeStruct(small.shape, F32),
        ],
        scratch_shapes=scratch,
        compiler_params=pltpu.CompilerParams(
            collective_id=4, has_side_effects=True, vmem_limit_bytes=56 << 20
        ),
        cost_estimate=pl.CostEstimate(
            flops=32 * rows * width * PAD, bytes_accessed=64 * rows * width, transcendentals=0
        ),
    )(grads, ones, head_full, grad_out, small, grad_hidden, tokens, gain[None])


def route_kernel(routes_ref, rows_ref, cols_ref, info_ref):
    tokens = routes_ref.shape[2]
    expert = lax.broadcasted_iota(jnp.int32, (NF, tokens), 0)
    step = 256
    down = lax.broadcasted_iota(jnp.int32, (step, step), 0)
    across = lax.broadcasted_iota(jnp.int32, (step, step), 1)
    before = jnp.where(down < across, 1.0, 0.0).astype(BF16)
    for a in range(2):
        hot = (expert == routes_ref[a, 0:1, :]) | (expert == routes_ref[a, 1:2, :])
        ones = jnp.where(hot, 1.0, 0.0)
        ranks, so_far = [], jnp.zeros((NF, 1), F32)
        for b in range(tokens // step):
            part = ones[:, b * step : (b + 1) * step]
            ranks.append(dot_nn(part.astype(BF16), before) + so_far)
            so_far = so_far + jnp.sum(part, axis=1, keepdims=True)
        rank = jnp.concatenate(ranks, axis=1)
        slots = jnp.where(hot, rank, -1.0)
        rows_ref[a] = slots.astype(jnp.int32)
        spread = jnp.concatenate([slots, jnp.zeros((128 - NF, tokens), F32)], axis=0)
        cols_ref[a] = spread.T.astype(jnp.int32)
        lane = lax.broadcasted_iota(jnp.int32, (NF, 128), 1)
        info = jnp.where(lane == 0, so_far, 0.0)
        for c in range(2):
            first = jnp.sum(jnp.where(rank + ones <= c * TILE, 1.0, 0.0), axis=1, keepdims=True)
            after = jnp.sum(jnp.where(rank < (c + 1) * TILE, 1.0, 0.0), axis=1, keepdims=True)
            info = jnp.where(lane == 1 + 2 * c, first, jnp.where(lane == 2 + 2 * c, after, info))
        info_ref[a] = info.astype(jnp.int32)


def route(routes):
    tokens = routes.shape[2]
    return pl.pallas_call(
        route_kernel,
        out_shape=[
            jax.ShapeDtypeStruct((2, NF, tokens), jnp.int32),
            jax.ShapeDtypeStruct((2, tokens, 128), jnp.int32),
            jax.ShapeDtypeStruct((2, NF, 128), jnp.int32),
        ],
        cost_estimate=pl.CostEstimate(flops=10**7, bytes_accessed=10**6, transcendentals=0),
    )(routes)


def experts_kernel(
    whole_weights, n_before, base_ref, info_ref, slot_rows_ref, slot_cols_ref, weights_ref, *refs
):
    (rows_in, grads_in), before, refs = refs[:2], refs[2 : 2 + n_before], refs[2 + n_before :]
    sums_out, grad_ins_out, out_ref, rows, grads, sums, grad_ins = refs[:7]
    weight, row_acc, grad_acc, slot_col, inputs, grad_outs, acts, gates, ups, in_sems, out_sems = refs[7:]
    step = pl.program_id(0)
    expert = base_ref[0] + step
    tokens, width = grads.shape[1:]
    wide = rows.shape[2]
    arrivals = [
        [pltpu.make_async_copy(rows_in.at[a], rows.at[a], in_sems.at[a, 0]),
         pltpu.make_async_copy(grads_in.at[a], grads.at[a], in_sems.at[a, 1])]
        + [pltpu.make_async_copy(source.at[a], target.at[a], in_sems.at[a, 2 + k])
           for k, (source, target) in enumerate(zip(before, (sums, grad_ins)))]
        for a in range(2)
    ]
    leaving = [
        [pltpu.make_async_copy(source.at[a], target.at[a], out_sems.at[a, k])
         for k, (source, target) in enumerate(((sums, sums_out), (grad_ins, grad_ins_out)))]
        for a in range(2)
    ]

    @pl.when(step == 0)
    def _():
        for copy in arrivals[0] + arrivals[1]:
            copy.start()
        if not n_before:
            sums[...] = jnp.zeros_like(sums)
            grad_ins[...] = jnp.zeros_like(grad_ins)

    if whole_weights:
        weight[...] = weights_ref[0]
    else:
        depth, _, _, _, share, _ = weights_ref.shape
        for z in range(depth):
            for y in range(2):
                weight[:, pl.ds((2 * z + y) * share, share), :] = weights_ref[z, y, 0]

    def tree(a):
        def dispatch(c, start, count):
            down = c * TILE + lax.broadcasted_iota(jnp.int32, (TILE, 1), 0)
            at = pl.ds(start, count)
            picked = slot_rows_ref[a, pl.ds(expert, 1), at] == down
            picked = jnp.where(picked, 1.0, 0.0).astype(BF16)
            row_acc[...] = dot_nn(picked, rows[a, at, :])
            grad_acc[...] = dot_nn(picked, grads[a, at, :])

        slot_col[...] = pltpu.roll(slot_cols_ref[a], 128 - expert, 1)

        def combine(c, start, count, back):
            across = c * TILE + lax.broadcasted_iota(jnp.int32, (1, TILE), 1)
            size = 256
            for b in range(count // size):
                at = pl.ds(pl.multiple_of(start + b * size, 128), size)
                here = jnp.where(slot_col[at, 0:1] == across, 1.0, 0.0).astype(BF16)
                part = dot_nn(here, back)
                sums[a, at, :] = (sums[a, at, :].astype(F32) + part[:, :width]).astype(BF16)
                grad_ins[a, at, :] = (
                    grad_ins[a, at, :].astype(F32) + part[:, width:]
                ).astype(BF16)

        def tile(c, carry):
            k = 8 * a + expert
            first, after = info_ref[k, 1 + 2 * c], info_ref[k, 2 + 2 * c]
            start = pl.multiple_of(jnp.minimum(first // 128 * 128, tokens - WINDOW), 128)
            narrow = after <= start + WINDOW

            @pl.when(narrow)
            def _():
                dispatch(c, start, WINDOW)

            @pl.when(jnp.logical_not(narrow))
            def _():
                dispatch(c, 0, tokens)

            at = pl.ds(pl.multiple_of((2 * a + c) * TILE, TILE), TILE)
            inputs[at, :] = row_acc[:, :width].astype(BF16)
            lane = lax.broadcasted_iota(jnp.int32, (TILE, wide - width), 1)
            gate = jnp.sum(
                jnp.where(lane == expert, row_acc[:, width:], 0.0), axis=1, keepdims=True
            )
            grad_out = (gate * grad_acc[...]).astype(BF16)
            grad_outs[at, :] = grad_out
            gate_part = dot_nn(inputs[at, :], weight[0])
            up_part = dot_nn(inputs[at, :], weight[1])
            sigmoid = 1.0 / (1.0 + jnp.exp(-gate_part))
            swish = gate_part * sigmoid
            act = (swish * up_part).astype(BF16)
            acts[at, :] = act
            expert_out = dot_nt(act, weight[2])
            along = jnp.sum(expert_out * grad_acc[...], axis=1, keepdims=True)
            grad_act = dot_nn(grad_out, weight[2])
            grad_gate = (
                grad_act * up_part * sigmoid * (1.0 + gate_part * (1.0 - sigmoid))
            ).astype(BF16)
            grad_up = (grad_act * swish).astype(BF16)
            gates[at, :] = grad_gate
            ups[at, :] = grad_up
            grad_in = dot_nt(grad_gate, weight[0]) + dot_nt(grad_up, weight[1])
            back = jnp.concatenate(
                [
                    (gate * expert_out).astype(BF16),
                    grad_in.astype(BF16),
                    jnp.where(lane == expert, along, 0.0).astype(BF16),
                ],
                axis=1,
            )

            @pl.when(narrow)
            def _():
                combine(c, start, WINDOW, back)

            @pl.when(jnp.logical_not(narrow))
            def _():
                combine(c, 0, tokens, back)

            return carry

        tiles = (info_ref[8 * a + expert, 0] + TILE - 1) // TILE

        def empty(c, carry):
            at = pl.ds(pl.multiple_of((2 * a + c) * TILE, TILE), TILE)
            for ref in (inputs, grad_outs, acts, gates, ups):
                ref[at, :] = jnp.zeros((TILE, ref.shape[1]), BF16)
            return carry

        lax.fori_loop(0, tiles, tile, 0)
        lax.fori_loop(tiles, 2, empty, 0)

    for a in range(2):

        @pl.when(step == 0)
        def _(a=a):
            for copy in arrivals[a]:
                copy.wait()

        tree(a)

        @pl.when(step == pl.num_programs(0) - 1)
        def _(a=a):
            for copy in leaving[a]:
                copy.start()

    for k, (left, right) in enumerate(((inputs, gates), (inputs, ups), (grad_outs, acts))):
        size = 256
        for b in range(width // size):
            at = slice(b * size, (b + 1) * size)
            if whole_weights:
                out_ref[0, k, at, :] = dot_tn(left[:, at], right[...]).astype(BF16)
            else:
                weight[k, at, :] = dot_tn(left[:, at], right[...]).astype(BF16)
    if not whole_weights:
        for z in range(depth):
            for y in range(2):
                out_ref[z, y, 0] = weight[:, pl.ds((2 * z + y) * share, share), :]

    @pl.when(step == pl.num_programs(0) - 1)
    def _():
        for copy in leaving[0] + leaving[1]:
            copy.wait()


def experts(base, weights, info, rows, grads, slot_rows, slot_cols, before):
    _, tokens, width = grads.shape
    wide = rows.shape[2]
    whole_weights = weights.ndim == 4
    kinds, share, hidden = weights.shape[-3:]
    group = weights.shape[0] if whole_weights else weights.shape[2]
    depth = width if whole_weights else 2 * weights.shape[0] * share
    whole = lambda a: pl.BlockSpec(a.shape, lambda e, *_: (0,) * a.ndim, pipeline_mode=pl.Buffered(1))
    anywhere = pl.BlockSpec(memory_space=pl.ANY)
    if whole_weights:
        weight_spec = pl.BlockSpec((1, kinds, share, hidden), lambda e, *_: (e, 0, 0, 0))
    else:
        weight_spec = pl.BlockSpec(
            (weights.shape[0], 2, 1, kinds, share, hidden), lambda e, *_: (0, 0, e, 0, 0, 0)
        )
    sums = jax.ShapeDtypeStruct((2, tokens, width), BF16)
    grad_ins = jax.ShapeDtypeStruct((2, tokens, wide), BF16)
    return pl.pallas_call(
        functools.partial(experts_kernel, whole_weights, len(before)),
        grid_spec=pltpu.PrefetchScalarGridSpec(
            num_scalar_prefetch=2,
            grid=(group,),
            in_specs=[whole(slot_rows), whole(slot_cols), weight_spec]
            + [anywhere] * (2 + len(before)),
            out_specs=[anywhere, anywhere, weight_spec],
            scratch_shapes=[
                pltpu.VMEM((2, tokens, wide), BF16),
                pltpu.VMEM((2, tokens, width), BF16),
                pltpu.VMEM((2, tokens, width), BF16),
                pltpu.VMEM((2, tokens, wide), BF16),
                pltpu.VMEM((kinds, depth, hidden), BF16),
                pltpu.VMEM((TILE, wide), F32),
                pltpu.VMEM((TILE, width), F32),
                pltpu.VMEM((tokens, 128), jnp.int32),
                pltpu.VMEM((4 * TILE, width), BF16),
                pltpu.VMEM((4 * TILE, width), BF16),
                pltpu.VMEM((4 * TILE, hidden), BF16),
                pltpu.VMEM((4 * TILE, hidden), BF16),
                pltpu.VMEM((4 * TILE, hidden), BF16),
                pltpu.SemaphoreType.DMA((2, 4)),
                pltpu.SemaphoreType.DMA((2, 2)),
            ],
        ),
        out_shape=[sums, grad_ins, jax.ShapeDtypeStruct(weights.shape, BF16)],
        compiler_params=pltpu.CompilerParams(vmem_limit_bytes=60 << 20),
        cost_estimate=pl.CostEstimate(
            flops=group * tokens * width * (9 * hidden + 4 * tokens),
            bytes_accessed=16 * tokens * width,
            transcendentals=0,
        ),
    )(base, info, slot_rows, slot_cols, weights, rows, grads, *before)


def per_device(
    tokens_in,
    carried_logits,
    cotangent,
    segment_ids,
    parent_ids,
    routes,
    attention_gain,
    head_weight,
    output_weight,
    expert_gain,
    router_weight,
    carry_weight,
    constant_gate,
    constant_vector,
    expert_first,
    expert_second,
):
    row_count, width = tokens_in.shape
    tree_len = segment_ids.shape[0]
    head_width = head_weight.shape[2]
    heads = head_width // HEAD
    share = head_weight.shape[1]
    parity = lax.axis_index("dp") % 2
    index = lax.axis_index("tensor")
    own_experts = NF // 2
    group = own_experts // GROUPS
    layered = share % 16 == 0

    columns = lax.axis_size("dp") == 8

    def gather_experts(shards):
        gathered = gather_column(shards)
        if layered:
            return gathered
        return gathered.transpose(2, 3, 0, 1, 4, 5).reshape(group, 3, width, -1)

    sections = jnp.concatenate([head_weight, output_weight.T[None]], axis=0).astype(BF16)
    spread = lambda a, to: jnp.pad(a, ((0, 0), (0, to - a.shape[1])))
    if columns:
        pack = jnp.concatenate(
            [sections[k, :, :128] for k in range(4)] + [sections[k, :, 128:] for k in range(4)], axis=1
        )
    else:
        pack = jnp.concatenate([spread(sections[k], PAD) for k in range(4)], axis=1)
        pack = gather_column(pack)
        pack = jnp.moveaxis(by_parity(pack, swap(pack, "dp", 1)), 0, 1).reshape(width, 4 * PAD)
    expert_pack = jnp.concatenate(
        [expert_first.astype(BF16), expert_second.astype(BF16).transpose(0, 2, 1)[:, None]], axis=1
    )
    kept = lax.dynamic_slice_in_dim(expert_pack, parity * own_experts, own_experts, 0)
    given = lax.dynamic_slice_in_dim(expert_pack, (1 - parity) * own_experts, own_experts, 0)
    first = slice(0, group)
    shards = by_parity(kept[first], swap(given[first], "dp", 1))
    pack, shards = together(pack, shards)
    expert_weights = [gather_experts(shards)]

    slot_rows, slot_cols, info = route(jnp.stack([routes.T, swap(routes.T, "dp", 1)]))
    info = info.reshape(2 * NF, -1)[:, :8]

    angles = rotary_angles(segment_ids, parent_ids)
    rowinfo = jnp.pad(jnp.stack([segment_ids, parent_ids]), ((0, 6), (0, 0)))
    colinfo = rowinfo.T
    queries, keys, values, keys_t, values_t, gathered_one, head_full = project(
        columns, tokens_in, attention_gain, angles, pack
    )
    queries, kept, given = together(queries, kept, given)
    shards = [
        by_parity(kept[at], swap(given[at], "dp", 1))
        for at in [slice(g * group, (g + 1) * group) for g in range(1, GROUPS)]
    ]
    expert_weights += [gather_experts(s) for s in shards]
    local_routes = lax.dynamic_slice_in_dim(routes, index * row_count, row_count, 0)
    picked = jnp.sum(
        (local_routes[:, :, None] == jnp.arange(128, dtype=jnp.int32)).astype(F32), axis=1
    )
    carried_part = spread(jnp.dot(carried_logits, carry_weight, precision=HIGHEST), 128)
    mix_weight = spread(jnp.concatenate([spread(router_weight, MIX), constant_gate], axis=1), 128)
    attended, totals, hidden, aux, expert_rows, grad_rows = branch(
        heads, queries, keys, values_t, rowinfo, colinfo, cotangent, head_full, tokens_in, expert_gain,
        carried_part, mix_weight, picked,
    )

    parts, own_grads = [], []
    for g in range(GROUPS):
        base = (parity * own_experts + g * group).astype(jnp.int32).reshape(1)
        *parts, weight_grads = experts(
            base, expert_weights[g], info, expert_rows, grad_rows, slot_rows, slot_cols, parts
        )
        if not layered:
            weight_grads = weight_grads.reshape(group, 3, -1, 2, share, weight_grads.shape[-1])
            weight_grads = weight_grads.transpose(2, 3, 0, 1, 4, 5)
        own_grads.append(scatter_column(weight_grads))
    sums, grad_ins = parts

    vectors = jnp.pad(constant_vector, ((0, 6), (0, 0)))
    grad_hidden, grad_logits, grad_output_t, small, grad_projected, output = branch_back(
        heads, hidden, aux, cotangent, expert_gain, mix_weight, vectors, spread(carried_logits, 128),
        attended, head_full, queries, keys, values, keys_t, rowinfo, colinfo, totals, angles, sums,
        grad_ins,
    )
    grad_carried = lax.dot_general(
        grad_logits[:, :NE], carry_weight, (((1,), (1,)), ((), ())), precision=HIGHEST
    )
    grad_projected, own_grads[0] = together(grad_projected, own_grads[0])
    grad_tokens, own_pack, small = finish(
        columns, grad_projected, gathered_one, head_full, grad_output_t, small, grad_hidden, tokens_in,
        attention_gain,
    )
    if columns:
        own_sections = [
            jnp.concatenate(
                [own_pack[:, 128 * k : 128 * (k + 1)], own_pack[:, 512 + 64 * k : 576 + 64 * k]], axis=1
            )
            for k in range(4)
        ]
    else:
        blocks = own_pack.reshape(-1, 2, share, 4 * PAD)
        kept = lax.dynamic_index_in_dim(blocks, parity, 1, keepdims=False)
        given = lax.dynamic_index_in_dim(blocks, 1 - parity, 1, keepdims=False)
        paired = kept.astype(F32) + swap(given, "dp", 1).astype(F32)
        own_pack = scatter_column(paired.astype(BF16)).astype(F32)
        own_sections = [own_pack[:, k * PAD : k * PAD + head_width] for k in range(4)]
        small = lax.psum(small, ("dp", "tensor"))
    own_grads = jnp.concatenate(own_grads, axis=1)
    kept = lax.dynamic_index_in_dim(own_grads, parity, 0, keepdims=False)
    given = lax.dynamic_index_in_dim(own_grads, 1 - parity, 0, keepdims=False)
    own_grads = by_parity(kept, swap(given, "dp", 1)).reshape(NF, 3, share, -1).astype(F32)
    grad_first = own_grads[:, :2]
    grad_second = own_grads[:, 2].transpose(0, 2, 1)
    return (
        output,
        grad_tokens,
        grad_carried,
        small[19, :width],
        jnp.stack(own_sections[:3]),
        own_sections[3].T,
        small[16, :width],
        small[:NE, :width].T,
        small[:NE, width : width + NE],
        small[MIX : MIX + 4, :width].T,
        small[17:19, :width],
        grad_first,
        grad_second,
    )


def solution(mesh):
    in_specs = (
        P(("dp", "tensor"), None),
        P(("dp", "tensor"), None),
        P(("dp", "tensor"), None),
        P("dp"),
        P("dp"),
        P("dp", None),
        P(),
        P(None, "dp", "tensor"),
        P("tensor", "dp"),
        P(),
        P(),
        P(),
        P(),
        P(),
        P(None, None, "dp", "tensor"),
        P(None, "tensor", "dp"),
    )
    out_specs = (
        P(("dp", "tensor"), None),
        P(("dp", "tensor"), None),
        P(("dp", "tensor"), None),
        P(),
        P(None, "dp", "tensor"),
        P("tensor", "dp"),
        P(),
        P(),
        P(),
        P(),
        P(),
        P(None, None, "dp", "tensor"),
        P(None, "tensor", "dp"),
    )
    return jax.shard_map(
        per_device, mesh=mesh, in_specs=in_specs, out_specs=out_specs, check_vma=False
    )
```

profile of v0, /device:TPU:2, one launch (start us, length us, event | category | flops | bytes accessed | tf_op | source)
XLA Modules:
  0.0 536.7 jit_solution(16032130471083884789)
XLA Ops:
  7.3 2.2 convert_element_type.32
  10.0 1.0 copy-done.11
  11.0 1.6 collective-permute-start
  12.6 1.0 convert.9
  13.8 0.8 concatenate.30.pack_ref
  14.5 11.6 %collective-permute-done = bf16[2,3,96,512]{3,2,1,0:T(8,128)(2,1)S(1)} collective-permute-done((bf16[2,3,96,512]{3,2,1,0:T(8,128)(2,1)S(1)}, bf16[2,3,96,512]{3,2,1,0:T(8,128)(2,1)S(1)}, u32[]{:S(2)}, u32[]{:S(2)}) %collective-permute-start) | collective-permute-done | bytes 589856 | tf_op jit(solution)/shard_map/ppermute | solution.py:75
  26.3 1.1 pad_maximum_fusion.1
  28.6 3.7 multiply_cosine_fusion
  32.3 1.3 pad_maximum_fusion.3.angle_ref
  33.6 42.8 %shard_map.255 = (bf16[2048,256]{1,0:T(8,128)(2,1)}, bf16[2048,256]{1,0:T(8,128)(2,1)}, bf16[2048,256]{1,0:T(8,128)(2,1)}, bf16[256,2048]{1,0:T(8,128)(2,1)}, bf...) custom-call(bf16[512,768]{1,0:T(8,128)(2,1)} %tok_ref.5, ...), custom_call_target="tpu_custom_call" | custom-call | flops 2415919104 | bytes 25165824 | tf_op jit(solution)/shard_map/pallas_call | solution.py:207
  76.9 10.4 %collective-permute-done.2 = bf16[2,3,96,512]{3,2,1,0:T(8,128)(2,1)S(1)} collective-permute-done((bf16[2,3,96,512]{3,2,1,0:T(8,128)(2,1)S(1)}, bf16[2,3,96,512]{3,2,1,0:T(8,128)(2,1)S(1)}, u32[]{:S(2)}, u32[]{:S(2)}) %collective-permute-start.2) | collective-permute-done | bytes 589856 | tf_op jit(solution)/shard_map/ppermute | solution.py:75
  87.3 1.1 pad_maximum_fusion.2
  88.7 1.6 collective-permute-start.1
  91.6 1.1 pad_bitcast_fusion.colinfo_ref
  94.0 2.9 shard_map.257
  96.9 1.0 slice.116.out_ref
  98.0 1.3 copy-done.7
  99.3 83.9 %shard_map.256 = (bf16[2048,256]{1,0:T(8,128)(2,1)S(1)}, f32[8,2048]{1,0:T(8,128)S(1)}, f32[512,768]{1,0:T(8,128)}, f32[512,128]{1,0:T(8,128)S(1)}, bf16[2,2048,...) custom-call(bf16[2048,256]{1,0:T(8,128)(2,1)S(1)} %copy-done.7, bf16[2048,256]{1,0:T(8,128)(2,1)} %get-tuple-element.54.k_ref, ...), custom_call_target="tpu_custom_call" | custom-call | flops 6442450944 | bytes 25165824 | tf_op jit(solution)/shard_map/pallas_call | solution.py:464
  183.3 1.0 copy-done.8
  184.3 0.7 copy-done.9
  185.0 62.9 %shard_map.258 = (bf16[2,2048,768]{2,1,0:T(8,128)(2,1)}, bf16[2,2048,896]{2,1,0:T(8,128)(2,1)}, bf16[4,2,2,3,96,512]{5,4,3,2,1,0:T(8,128)(2,1)}) custom-call(s32[1]{0:T(128)} %bitcast.29.base_ref, s32[16,8]{1,0:T(8,128)} %bitcast.105, s32[2,8,2048]{2,1,0:T(8,128)} %get-tuple-element.64.slot_rows_ref, s32[2,2048,128]{2,1,0:T(8,128)} %get-tuple-element.65.slot_cols_ref, ...), custom_call_target="tpu_custom_call" | custom-call | flops 40265318400 | bytes 25165824 | tf_op jit(solution)/shard_map/pallas_call | solution.py:1205
  248.0 59.7 %shard_map.259 = (bf16[2,2048,768]{2,1,0:T(8,128)(2,1)}, bf16[2,2048,896]{2,1,0:T(8,128)(2,1)}, bf16[4,2,2,3,96,512]{5,4,3,2,1,0:T(8,128)(2,1)}) custom-call(s32[1]{0:T(128)} %bitcast.21.base_ref, s32[16,8]{1,0:T(8,128)} %bitcast.106, s32[2,8,2048]{2,1,0:T(8,128)} %get-tuple-element.64.slot_rows_ref, s32[2,2048,128]{2,1,0:T(8,128)} %get-tuple-element.65.slot_cols_ref, ...), custom_call_target="tpu_custom_call" | custom-call | flops 40265318400 | bytes 25165824 | tf_op jit(solution)/shard_map/pallas_call | solution.py:1205
  307.9 0.7 pad.23.carried_ref
  309.3 107.0 %shard_map.260 = (f32[512,768]{1,0:T(8,128)}, f32[512,128]{1,0:T(8,128)}, f32[768,256]{1,0:T(8,128)}, f32[24,896]{1,0:T(8,128)}, bf16[2048,768]{1,0:T(8,128)(2,1)}, /*index=5*/bf16[512,768]{1,0:T(8,128)(2,1)}) custom-call(f32[512,768]{1,0:T(8,128)} %get-tuple-element.57.hidden_ref, f32[512,128]{1,0:T(8,128)} %copy-done.9, bf16[512,768]{1,0:T(8,128)(2,1)} %cot_ref.3, ...), custom_call_target="tpu_custom_call" | custom-call | flops 25769803776 | bytes 25165824 | tf_op jit(solution)/shard_map/pallas_call | solution.py:782
  416.3 1.9 fusion.6
  418.3 73.6 %shard_map.261 = (f32[512,768]{1,0:T(8,128)}, f32[96,768]{1,0:T(8,128)}, f32[24,896]{1,0:T(8,128)}) custom-call(bf16[2048,768]{1,0:T(8,128)(2,1)} %get-tuple-element.78.grad_ref, bf16[2048,768]{1,0:T(8,128)(2,1)} %get-tuple-element.79.one_ref, bf16[768,1024]{1,0:T(8,128)(2,1)} %get-tuple-element.56.head_ref, f32[768,256]{1,0:T(8,128)} %get-tuple-element.80.grad_out_ref, ...), custom_call_target="tpu_custom_call" | custom-call | flops 3221225472 | bytes 25165824 | tf_op jit(solution)/shard_map/pallas_call | solution.py:964
  491.9 1.5 fusion.8
  493.4 2.2 fusion.3
  495.7 0.9 collective-permute-start.3
  496.5 0.7 fusion.9
  497.3 1.3 slice.132
  498.6 1.3 slice.134
  499.9 0.7 maximum_bitcast_fusion.3
  500.5 1.6 copy.82
  502.2 1.4 slice_reduce_fusion
  503.6 0.8 maximum_bitcast_fusion
  504.4 0.8 maximum_bitcast_fusion.1
  505.3 0.8 maximum_bitcast_fusion.2
  506.1 0.7 pad_maximum_fusion.4
  506.9 1.3 slice_bitcast_fusion.10
  508.2 1.4 slice_bitcast_fusion.1
  509.6 12.9 %collective-permute-done.3 = bf16[4,3,96,512]{3,2,1,0:T(8,128)(2,1)S(1)} collective-permute-done((bf16[4,3,96,512]{3,2,1,0:T(8,128)(2,1)}, bf16[4,3,96,512]{3,2,1,0:T(8,128)(2,1)S(1)}, u32[]{:S(2)}, u32[]{:S(2)}) %collective-permute-start.3) | collective-permute-done | bytes 1179680 | tf_op jit(solution)/shard_map/ppermute | solution.py:75
  522.9 0.8 bitcast_convert_fusion
  523.7 2.0 slice.148
  525.8 1.3 slice_bitcast_fusion
  527.1 0.9 copy.88
  528.0 0.8 copy-done.16
  528.8 1.1 copy.89
  (104 shorter events, 6.4 us)
Async XLA Ops:
  7.2 83.8 %copy-start = (f32[12,12]{1,0:T(8,128)S(1)}, f32[12,12]{1,0:T(8,128)}, u32[]{:S(2)}) copy-start(f32[12,12]{1,0:T(8,128)} %param.27) | copy-start | bytes 1732
  7.2 177.8 %all-gather.7.cloned.1.call-start = ((), (), s32[]{:S(2)}) async-start(), calls=%async_computation.5 | async-start | bytes 5898240 | tf_op jit(solution)/shard_map/all_gather | solution.py:88
  7.3 2.4 copy-start.15
  10.0 1.0 copy-start.11
  10.0 3.6 copy-start.22
  11.0 15.1 %collective-permute-start = (bf16[2,3,96,512]{3,2,1,0:T(8,128)(2,1)S(1)}, bf16[2,3,96,512]{3,2,1,0:T(8,128)(2,1)S(1)}, u32[]{:S(2)}, u32[]{:S(2)}) collective-permute-start(bf16[2,3,96,512]{3,2,1,0:T(8,128)(2,1)S(1)} %slice.146), channel_id=1, source_target_pairs={{0,4},{4,0},{8,12},{12,8},{16,20},{20,16},{24,28},{28,24},{1,5},{5... | collective-permute-start | bytes 1769480 | tf_op jit(solution)/shard_map/ppermute | solution.py:75
  26.2 1.2 copy-start.21
  26.3 1.6 copy-start.28
  26.3 2.1 copy-start.23
  27.4 220.6 %all-gather.5.cloned.1.call-start = ((), (), s32[]{:S(2)}) async-start(), calls=%async_computation.4 | async-start | bytes 5898240 | tf_op jit(solution)/shard_map/all_gather | solution.py:88
  33.6 42.8 %copy-start.12 = (bf16[4,3,96,512]{3,2,1,0:T(8,128)(2,1)S(1)}, bf16[4,3,96,512]{3,2,1,0:T(8,128)(2,1)}, u32[]{:S(2)}) copy-start(bf16[4,3,96,512]{3,2,1,0:T(8,128)(2,1)} %copy-done.11) | copy-start | bytes 3538948
  76.5 10.8 %collective-permute-start.2 = (bf16[2,3,96,512]{3,2,1,0:T(8,128)(2,1)S(1)}, bf16[2,3,96,512]{3,2,1,0:T(8,128)(2,1)S(1)}, u32[]{:S(2)}, u32[]{:S(2)}) collective-permute-start(bf16[2,3,96,512]{3,2,1,0:T(8,128)(2,1)S(1)} %slice.119), channel_id=1, source_target_pairs={{0,4},{4,0},{8,12},{12,8},{16,20},{20,16},{24,28},{28,24},{1,5},{5... | collective-permute-start | bytes 1769480 | tf_op jit(solution)/shard_map/ppermute | solution.py:75
  87.3 1.4 copy-start.25
  88.5 2.6 copy-start.20
  88.5 329.8 %reduce-scatter.3.cloned.1.call-start = ((), (), s32[]{:S(2)}) async-start(), calls=%async_computation.2 | async-start | bytes 5898240 | tf_op jit(solution)/shard_map/reduce_scatter | solution.py:92
  88.7 4.7 collective-permute-start.1
  90.8 2.0 copy-start.24
  90.8 2.0 copy-start.26
  91.6 1.6 copy-start.29
  93.1 4.9 copy-start.5
  93.1 4.9 copy-start.6
  93.1 90.1 %copy-start.3 = (s32[8,2048]{1,0:T(8,128)}, s32[8,2048]{1,0:T(8,128)S(1)}, u32[]{:S(2)}) copy-start(s32[8,2048]{1,0:T(8,128)S(1)} %pad.19.clone.rowinfo_ref) | copy-start | bytes 196612
  93.3 89.9 %copy-start.4 = (f32[1,768]{1,0:T(1,128)}, f32[1,768]{1,0:T(1,128)S(1)}, u32[]{:S(2)}) copy-start(f32[1,768]{1,0:T(1,128)S(1)} %broadcast_in_dim.21.gain_ref) | copy-start | bytes 9220
  93.3 89.9 %copy-start.2 = (f32[768,128]{1,0:T(8,128)}, f32[768,128]{1,0:T(8,128)S(1)}, u32[]{:S(2)}) copy-start(f32[768,128]{1,0:T(8,128)S(1)} %pad.21.mix_ref) | copy-start | bytes 1179652
  97.9 85.3 %copy-start.1 = (bf16[768,256]{1,0:T(8,128)(2,1)}, bf16[768,256]{1,0:T(8,128)(2,1)S(1)}, u32[]{:S(2)}) copy-start(bf16[768,256]{1,0:T(8,128)(2,1)S(1)} %slice.116.out_ref) | copy-start | bytes 1179652
  98.0 1.4 copy-start.7
  183.3 1.0 copy-start.8
  184.3 0.7 copy-start.9
  185.0 63.0 %copy-start.10 = (f32[8,2048]{1,0:T(8,128)}, f32[8,2048]{1,0:T(8,128)S(1)}, u32[]{:S(2)}) copy-start(f32[8,2048]{1,0:T(8,128)S(1)} %get-tuple-element.62.total_ref) | copy-start | bytes 196612
  248.0 245.4 %reduce-scatter.5.cloned.1.call-start = ((), (), s32[]{:S(2)}) async-start(), calls=%async_computation.3 | async-start | bytes 5898240 | tf_op jit(solution)/shard_map/reduce_scatter | solution.py:92
  307.8 0.9 copy-start.27
  418.2 75.2 %copy-start.13 = (bf16[1,2,2,3,96,512]{5,4,3,2,1,0:T(8,128)(2,1)S(1)}, bf16[1,2,2,3,96,512]{5,4,3,2,1,0:T(8,128)(2,1)}, u32[]{:S(2)}) copy-start(bf16[1,2,2,3,96,512]{5,4,3,2,1,0:T(8,128)(2,1)} %reduce-scatter.3.cloned.1.call-done) | copy-start | bytes 3538948
  493.4 3.1 copy-start.18
  493.4 6.5 %copy-start.19 = (f32[96,128]{1,0:T(8,128)S(1)}, f32[96,128]{1,0:T(8,128)}, u32[]{:S(2)}) copy-start(f32[96,128]{1,0:T(8,128)} %get-tuple-element.164) | copy-start | bytes 147460
  495.6 26.9 %copy-start.14 = (bf16[1,2,2,3,96,512]{5,4,3,2,1,0:T(8,128)(2,1)S(1)}, bf16[1,2,2,3,96,512]{5,4,3,2,1,0:T(8,128)(2,1)}, u32[]{:S(2)}) copy-start(bf16[1,2,2,3,96,512]{5,4,3,2,1,0:T(8,128)(2,1)} %reduce-scatter.5.cloned.1.call-done) | copy-start | bytes 3538948
  495.7 26.9 %collective-permute-start.3 = (bf16[4,3,96,512]{3,2,1,0:T(8,128)(2,1)}, bf16[4,3,96,512]{3,2,1,0:T(8,128)(2,1)S(1)}, u32[]{:S(2)}, u32[]{:S(2)}) collective-permute-start(bf16[4,3,96,512]{3,2,1,0:T(8,128)(2,1)} %fusion.3), channel_id=1, source_target_pairs={{0,4},{4,0},{8,12},{12,8},{16,20},{20,16},{24,28},{28,24},{1,5},{5... | collective-permute-start | bytes 3538952 | tf_op jit(solution)/shard_map/ppermute | solution.py:75
  525.8 1.3 copy-start.17
  527.1 1.7 copy-start.16
Sparse Core Ops, SparseCore 0:
  27.5 100.7 all-gather.6
  130.5 89.2 all-gather.4
  248.1 97.2 reduce-scatter.2
  347.5 85.7 reduce-scatter.4
where the time goes:
time: 546 us; the launch traced here: 537 us
  Pallas kernels  433 us (79%)
  waiting for transfers between devices  35 us (6%)
  local copies, waits for them, and re-layouts  27.2 us (5%)
  other arithmetic  19.6 us (4%)
  between operations  14.6 us (3%)
    pallas_call x2, Pallas kernels, experts(): pl.pallas_call(functools.partial(experts_kernel, whole_weights, len(befor...  123 us
    pallas_call x1, Pallas kernels, branch_back(): pl.pallas_call(functools.partial(branch_back_kernel, heads), in_specs=[vm...  107 us
    pallas_call x1, Pallas kernels, branch(): pl.pallas_call(functools.partial(branch_kernel, heads), in_specs=[vmem] *...  83.9 us
    pallas_call x1, Pallas kernels, finish(): pl.pallas_call(functools.partial(finish_kernel, columns), in_specs=[vmem]...  73.6 us
    pallas_call x1, Pallas kernels, project(): pl.pallas_call(functools.partial(project_kernel, columns), in_specs=[vmem...  42.8 us
    ppermute x4, waiting for transfers between devices, swap(): return lax.ppermute(values, axis, [(i, i ^ bits) for i in range(size)])  34.9 us
  transfers between devices with their start and end apart: 8, of which 3 were waited for; matrix products, arithmetic and copies ran while one was open for 6% of the time, Pallas kernels for 81%

commit v1 on v0

--- a/solution.py
+++ b/solution.py
@@ -12,7 +12,7 @@
 NSEG = 13
 NE = 12
 PAD = 256
-BLOCK = 256
+BLOCK = 512
 SLICES = 4
 MIX = 12
 WINDOW = 1280
@@ -124,9 +124,11 @@
 
 
 def project_kernel(columns, tok_ref, gain_ref, angle_ref, pack_ref, *refs):
+    if columns:
+        given_ref, refs = refs[0], refs[1:]
     q_ref, k_ref, v_ref, kt_ref, vt_ref, one_ref = refs[:6]
     if columns:
-        head_ref, gathered, shards, send_sems, recv_sems = refs[6:]
+        head_ref, received_ref, gathered, shards, send_sems, recv_sems = refs[6:]
     else:
         head_ref, (gathered, send_sems, recv_sems) = pack_ref, refs[6:]
     near, far, across, *column = enter(columns)
@@ -156,6 +158,7 @@
             heads[c].wait_recv()
             origin = lax.rem(dp + 8 - 2 * (c + 1), 8)
             last.append(copies.start(shards.at[origin], shards.at[origin], across))
+    beside = [copies.start(given_ref, received_ref, across)] if columns else []
     for move in last + near_moves + corner_moves:
         move.wait_recv()
     if columns:
@@ -189,26 +192,32 @@
         part = dot_nn(values, head_ref[:, 2 * PAD : 3 * PAD])
         v_ref[at, :] = part.astype(BF16)
         vt_ref[:, at] = part.T.astype(BF16)
+    for move in beside:
+        move.wait_recv()
     copies.finish()
 
 
-def project(columns, tokens, gain, angles, pack):
+def project(columns, tokens, gain, angles, pack, given):
     rows, width = tokens.shape
     total = angles.shape[0]
     vmem = pl.BlockSpec(memory_space=pltpu.VMEM)
-    copies = 3 * SLICES + 7
+    copies = 3 * SLICES + 8
+    anywhere = pl.BlockSpec(memory_space=pl.ANY)
     wide = jax.ShapeDtypeStruct((total, PAD), BF16)
     tall = jax.ShapeDtypeStruct((PAD, total), BF16)
     shapes = [wide, wide, wide, tall, tall, jax.ShapeDtypeStruct((total, width), BF16)]
     scratch = [pltpu.VMEM((4, rows, width), BF16)]
+    arguments, extra = [tokens, gain[None], angles, pack], []
     if columns:
         shapes.append(jax.ShapeDtypeStruct((width, 4 * PAD), BF16))
         scratch.append(pltpu.VMEM((8, *pack.shape), BF16))
+        arguments.append(given)
+        extra.append(jax.ShapeDtypeStruct(given.shape, BF16))
     out = pl.pallas_call(
         functools.partial(project_kernel, columns),
-        in_specs=[vmem] * 4,
-        out_specs=[vmem] * len(shapes),
-        out_shape=shapes,
+        in_specs=[vmem] * 4 + [anywhere] * len(extra),
+        out_specs=[vmem] * len(shapes) + [anywhere] * len(extra),
+        out_shape=shapes + extra,
         scratch_shapes=scratch
         + [pltpu.SemaphoreType.DMA((copies,)), pltpu.SemaphoreType.DMA((copies,))],
         compiler_params=pltpu.CompilerParams(
@@ -217,8 +226,8 @@
         cost_estimate=pl.CostEstimate(
             flops=6 * total * width * PAD, bytes_accessed=16 * total * width, transcendentals=0
         ),
-    )(tokens, gain[None], angles, pack)
-    return out if columns else [*out, pack]
+    )(*arguments)
+    return out if columns else [*out, pack, swap(given, "dp", 1)]
 
 
 def head_mask(values, head):
@@ -382,7 +391,7 @@
     near, far, _ = devices
     copies = Copies(send_sems, recv_sems)
     rows, width = tok_ref.shape
-    weights = out_ref[...]
+    weights = out_ref[:, 3 * PAD :]
     size = rows // SLICES
     slices = [pl.ds(c * size, size) for c in range(SLICES)]
     locals_ = [pltpu.make_async_copy(cot_ref, quarter(cots_ref.at[0], 0, rows), local_sems.at[0])]
@@ -490,7 +499,7 @@
             flops=64 * rows * width * PAD, bytes_accessed=64 * rows * width, transcendentals=0
         ),
     )(
-        queries, keys, values_t, rowinfo, colinfo, cotangent, head_full[:, 3 * PAD :], tokens, gain[None],
+        queries, keys, values_t, rowinfo, colinfo, cotangent, head_full, tokens, gain[None],
         carried, mix, picked,
     )
 
@@ -727,7 +736,7 @@
 
     def attention_back(bits):
         values = gathered[bits]
-        quarter(grad_att, bits, rows)[...] = dot_nn(values, out_ref[...]).astype(BF16)
+        quarter(grad_att, bits, rows)[...] = dot_nn(values, out_ref[:, 3 * PAD :]).astype(BF16)
         product = dot_tn(values, quarter(att_ref, bits, rows)[...])
         grad_out_ref[...] = grad_out_ref[...] + product if bits else product
         place = other(lax.axis_index("tensor"), bits)
@@ -812,7 +821,7 @@
             flops=256 * rows * width * PAD, bytes_accessed=64 * rows * width, transcendentals=0
         ),
     )(
-        hidden, aux, cotangent, gain[None], mix, vectors, carried, attended, head_full[:, 3 * PAD :],
+        hidden, aux, cotangent, gain[None], mix, vectors, carried, attended, head_full,
         queries, keys, values, keys_t, rowinfo, colinfo, totals, angles, sums, grad_ins,
     )
 
@@ -821,6 +830,8 @@
     columns, grad_ref, one_ref, head_ref, grad_out_ref, small_ref, grad_hidden_ref, tok_ref, gain_ref,
     *refs
 ):
+    if columns:
+        given_ref, received_ref, refs = refs[0], refs[4], refs[1:4] + refs[5:]
     grad_tok_ref, pack_ref, sum_ref, refs = refs[0], refs[1], refs[2], refs[3:]
     near_send, near_recv, far_send, far_recv, send_sems, recv_sems = refs[:6]
     near, far, across, *column = enter(columns)
@@ -883,6 +894,7 @@
         for j in range(4):
             there = lax.rem(other(dp, 1) + 2 * j, 8)
             pair_moves.append(copies.start(packed.at[there], pair_recv.at[j], across))
+        beside = copies.start(given_ref, received_ref, across)
         sums[0] = small
         steps = [near, far, across, (other(dp, 2), lax.axis_index("tensor")), column[1]]
         sum_moves = [copies.start(sums.at[0], sum_recv.at[0], steps[0])]
@@ -931,14 +943,16 @@
             column_moves[j].wait_recv()
             pack_ref[...] = pack_ref[...] + column_recv[j].astype(F32)
         add_up()
+        beside.wait_recv()
     copies.finish()
 
 
-def finish(columns, grads, ones, head_full, grad_out, small, grad_hidden, tokens, gain):
+def finish(columns, grads, ones, head_full, grad_out, small, grad_hidden, tokens, gain, given):
     rows, width = tokens.shape
     share = width // 8
     vmem = pl.BlockSpec(memory_space=pltpu.VMEM)
-    copies = 2 + SLICES + 12
+    copies = 2 + SLICES + 13
+    anywhere = pl.BlockSpec(memory_space=pl.ANY)
     pack = (
         jax.ShapeDtypeStruct((share, width), F32)
         if columns
@@ -961,15 +975,17 @@
             pltpu.VMEM((5, *small.shape), F32),
             pltpu.VMEM((5, *small.shape), F32),
         ]
-    return pl.pallas_call(
+    extra = [given] if columns else []
+    out = pl.pallas_call(
         functools.partial(finish_kernel, columns),
-        in_specs=[vmem] * 8,
-        out_specs=[vmem] * 3,
+        in_specs=[vmem] * 8 + [anywhere] * len(extra),
+        out_specs=[vmem] * 3 + [anywhere] * len(extra),
         out_shape=[
             jax.ShapeDtypeStruct((rows, width), F32),
             pack,
             jax.ShapeDtypeStruct(small.shape, F32),
-        ],
+        ]
+        + [jax.ShapeDtypeStruct(a.shape, a.dtype) for a in extra],
         scratch_shapes=scratch,
         compiler_params=pltpu.CompilerParams(
             collective_id=4, has_side_effects=True, vmem_limit_bytes=56 << 20
@@ -977,7 +993,8 @@
         cost_estimate=pl.CostEstimate(
             flops=32 * rows * width * PAD, bytes_accessed=64 * rows * width, transcendentals=0
         ),
-    )(grads, ones, head_full, grad_out, small, grad_hidden, tokens, gain[None])
+    )(grads, ones, head_full, grad_out, small, grad_hidden, tokens, gain[None], *extra)
+    return out if columns else [*out, swap(given, "dp", 1)]
 
 
 def route_kernel(routes_ref, rows_ref, cols_ref, info_ref):
@@ -1152,19 +1169,25 @@
         lax.fori_loop(0, tiles, tile, 0)
         lax.fori_loop(tiles, 2, empty, 0)
 
-    for a in range(2):
-
-        @pl.when(step == 0)
-        def _(a=a):
-            for copy in arrivals[a]:
-                copy.wait()
+    def one_tree(a, carry):
+        for k in range(2):
+
+            @pl.when(jnp.logical_and(step == 0, a == k))
+            def _(k=k):
+                for copy in arrivals[k]:
+                    copy.wait()
 
         tree(a)
-
-        @pl.when(step == pl.num_programs(0) - 1)
-        def _(a=a):
-            for copy in leaving[a]:
-                copy.start()
+        for k in range(2):
+
+            @pl.when(jnp.logical_and(step == pl.num_programs(0) - 1, a == k))
+            def _(k=k):
+                for copy in leaving[k]:
+                    copy.start()
+
+        return carry
+
+    lax.fori_loop(0, 2, one_tree, 0)
 
     for k, (left, right) in enumerate(((inputs, gates), (inputs, ups), (grad_outs, acts))):
         size = 256
@@ -1290,32 +1313,38 @@
     )
     kept = lax.dynamic_slice_in_dim(expert_pack, parity * own_experts, own_experts, 0)
     given = lax.dynamic_slice_in_dim(expert_pack, (1 - parity) * own_experts, own_experts, 0)
-    first = slice(0, group)
-    shards = by_parity(kept[first], swap(given[first], "dp", 1))
-    pack, shards = together(pack, shards)
-    expert_weights = [gather_experts(shards)]
-
-    slot_rows, slot_cols, info = route(jnp.stack([routes.T, swap(routes.T, "dp", 1)]))
+    cut = lambda a, g: a[g * group : (g + 1) * group]
+    shards = by_parity(cut(kept, 0), swap(cut(given, 0), "dp", 1))
+
+    routes_both = jnp.stack([routes.T, swap(routes.T, "dp", 1)])
+    slot_rows, slot_cols, info = route(routes_both)
     info = info.reshape(2 * NF, -1)[:, :8]
-
     angles = rotary_angles(segment_ids, parent_ids)
     rowinfo = jnp.pad(jnp.stack([segment_ids, parent_ids]), ((0, 6), (0, 0)))
     colinfo = rowinfo.T
-    queries, keys, values, keys_t, values_t, gathered_one, head_full = project(
-        columns, tokens_in, attention_gain, angles, pack
-    )
-    queries, kept, given = together(queries, kept, given)
-    shards = [
-        by_parity(kept[at], swap(given[at], "dp", 1))
-        for at in [slice(g * group, (g + 1) * group) for g in range(1, GROUPS)]
-    ]
-    expert_weights += [gather_experts(s) for s in shards]
     local_routes = lax.dynamic_slice_in_dim(routes, index * row_count, row_count, 0)
     picked = jnp.sum(
         (local_routes[:, :, None] == jnp.arange(128, dtype=jnp.int32)).astype(F32), axis=1
     )
     carried_part = spread(jnp.dot(carried_logits, carry_weight, precision=HIGHEST), 128)
     mix_weight = spread(jnp.concatenate([spread(router_weight, MIX), constant_gate], axis=1), 128)
+    vectors = jnp.pad(constant_vector, ((0, 6), (0, 0)))
+    (
+        pack, shards, slot_rows, slot_cols, info, rowinfo, colinfo, picked, carried_part, mix_weight,
+        vectors,
+    ) = together(
+        pack, shards, slot_rows, slot_cols, info, rowinfo, colinfo, picked, carried_part, mix_weight,
+        vectors,
+    )
+    expert_weights = [gather_experts(shards)]
+
+    queries, keys, values, keys_t, values_t, gathered_one, head_full, received = project(
+        columns, tokens_in, attention_gain, angles, pack, given[group:]
+    )
+    for g in range(1, GROUPS):
+        shards = by_parity(cut(kept, g), cut(received, g - 1))
+        queries, shards = together(queries, shards)
+        expert_weights.append(gather_experts(shards))
     attended, totals, hidden, aux, expert_rows, grad_rows = branch(
         heads, queries, keys, values_t, rowinfo, colinfo, cotangent, head_full, tokens_in, expert_gain,
         carried_part, mix_weight, picked,
@@ -1333,7 +1362,6 @@
         own_grads.append(scatter_column(weight_grads))
     sums, grad_ins = parts
 
-    vectors = jnp.pad(constant_vector, ((0, 6), (0, 0)))
     grad_hidden, grad_logits, grad_output_t, small, grad_projected, output = branch_back(
         heads, hidden, aux, cotangent, expert_gain, mix_weight, vectors, spread(carried_logits, 128),
         attended, head_full, queries, keys, values, keys_t, rowinfo, colinfo, totals, angles, sums,
@@ -1342,10 +1370,12 @@
     grad_carried = lax.dot_general(
         grad_logits[:, :NE], carry_weight, (((1,), (1,)), ((), ())), precision=HIGHEST
     )
+    mine = lambda a: lax.dynamic_index_in_dim(a, parity, 0, keepdims=False)
+    theirs = lambda a: lax.dynamic_index_in_dim(a, 1 - parity, 0, keepdims=False)
     grad_projected, own_grads[0] = together(grad_projected, own_grads[0])
-    grad_tokens, own_pack, small = finish(
+    grad_tokens, own_pack, small, received = finish(
         columns, grad_projected, gathered_one, head_full, grad_output_t, small, grad_hidden, tokens_in,
-        attention_gain,
+        attention_gain, theirs(own_grads[0]),
     )
     if columns:
         own_sections = [
@@ -1362,10 +1392,9 @@
         own_pack = scatter_column(paired.astype(BF16)).astype(F32)
         own_sections = [own_pack[:, k * PAD : k * PAD + head_width] for k in range(4)]
         small = lax.psum(small, ("dp", "tensor"))
-    own_grads = jnp.concatenate(own_grads, axis=1)
-    kept = lax.dynamic_index_in_dim(own_grads, parity, 0, keepdims=False)
-    given = lax.dynamic_index_in_dim(own_grads, 1 - parity, 0, keepdims=False)
-    own_grads = by_parity(kept, swap(given, "dp", 1)).reshape(NF, 3, share, -1).astype(F32)
+    kept = jnp.concatenate([mine(a) for a in own_grads], axis=0)
+    received = jnp.concatenate([received] + [swap(theirs(a), "dp", 1) for a in own_grads[1:]], axis=0)
+    own_grads = by_parity(kept, received).reshape(NF, 3, share, -1).astype(F32)
     grad_first = own_grads[:, :2]
     grad_second = own_grads[:, 2].transpose(0, 2, 1)
     return (

time: 546 us -> 495 us (0.907)
  the two profiles are of different devices: /device:TPU:2 before, /device:TPU:0 now
where the time goes in v1:
time: 495 us; the launch traced here: 488 us
  Pallas kernels  406 us (82%)
  local copies, waits for them, and re-layouts  31.4 us (6%)
  waiting for transfers between devices  14.9 us (3%)
  between operations  14.6 us (3%)
  other arithmetic  14.4 us (3%)
    pallas_call x1, Pallas kernels, branch_back(): pl.pallas_call(functools.partial(branch_back_kernel, heads), in_specs=[vm...  107 us
    pallas_call x2, Pallas kernels, experts(): pl.pallas_call(functools.partial(experts_kernel, whole_weights, len(befor...  105 us
    pallas_call x1, Pallas kernels, branch(): pl.pallas_call(functools.partial(branch_kernel, heads), in_specs=[vmem] *...  80.4 us
    pallas_call x1, Pallas kernels, finish(): pl.pallas_call(functools.partial(finish_kernel, columns), in_specs=[vmem]...  66.3 us
    pallas_call x1, Pallas kernels, project(): pl.pallas_call(functools.partial(project_kernel, columns), in_specs=[vmem...  44.4 us
    ppermute x3, waiting for transfers between devices, swap(): return lax.ppermute(values, axis, [(i, i ^ bits) for i in range(size)])  14.8 us
  transfers between devices with their start and end apart: 7, of which 2 were waited for; matrix products, arithmetic and copies ran while one was open for 6% of the time, Pallas kernels for 83%

profile of v1, /device:TPU:0, one launch (start us, length us, event | category | flops | bytes accessed | tf_op | source)
XLA Modules:
  0.0 488.1 jit_solution(1311324212153879842)
XLA Ops:
  7.3 2.2 convert_element_type.32
  10.0 1.1 fusion.4
  11.2 3.0 collective-permute-start
  14.8 1.5 pad_bitcast_fusion
  16.5 0.6 fusion.7
  17.4 0.7 pad.22.vector_ref
  18.1 0.8 concatenate.67.pack_ref
  18.9 9.1 %collective-permute-done.1 = s32[2,2048]{1,0:T(2,128)S(1)} collective-permute-done((s32[2,2048]{1,0:T(2,128)S(1)}, s32[2,2048]{1,0:T(2,128)S(1)}, u32[]{:S(2)}, u32[]{:S(2)}) %collective-permute-start.1) | collective-permute-done | bytes 16416 | tf_op jit(solution)/shard_map/ppermute | solution.py:75
  28.0 0.6 pad_add_fusion.routes_ref
  28.6 2.9 shard_map.255
  31.6 1.1 pad_maximum_fusion.1
  33.3 0.6 broadcast_in_dim.17.gain_ref
  34.1 3.7 multiply_cosine_fusion
  37.8 1.3 pad_maximum_fusion.5.angle_ref
  39.1 44.4 %shard_map.256 = (bf16[2048,256]{1,0:T(8,128)(2,1)}, bf16[2048,256]{1,0:T(8,128)(2,1)}, bf16[2048,256]{1,0:T(8,128)(2,1)}, bf16[256,2048]{1,0:T(8,128)(2,1)}, bf...) custom-call(bf16[512,768]{1,0:T(8,128)(2,1)} %tok_ref.5, ...), custom_call_target="tpu_custom_call" | custom-call | flops 2415919104 | bytes 25165824 | tf_op jit(solution)/shard_map/pallas_call | solution.py:216
  83.5 1.2 select_bitcast_fusion.1
  84.7 1.1 pad_maximum_fusion.2
  85.9 1.6 copy.75.rowinfo_ref
  87.6 1.3 copy-done.6
  88.8 1.2 copy-done.7
  90.1 80.4 %shard_map.257 = (bf16[2048,256]{1,0:T(8,128)(2,1)S(1)}, f32[8,2048]{1,0:T(8,128)S(1)}, f32[512,768]{1,0:T(8,128)}, f32[512,128]{1,0:T(8,128)S(1)}, bf16[2,2048,...) custom-call(bf16[2048,256]{1,0:T(8,128)(2,1)S(1)} %copy-done.6, bf16[2048,256]{1,0:T(8,128)(2,1)S(1)} %copy-done.7, ...), custom_call_target="tpu_custom_call" | custom-call | flops 6442450944 | bytes 25165824 | tf_op jit(solution)/shard_map/pallas_call | solution.py:473
  170.5 1.0 copy-done.8
  171.5 0.7 copy-done.9
  172.2 53.6 %shard_map.258 = (bf16[2,2048,768]{2,1,0:T(8,128)(2,1)}, bf16[2,2048,896]{2,1,0:T(8,128)(2,1)}, bf16[4,2,2,3,96,512]{5,4,3,2,1,0:T(8,128)(2,1)}) custom-call(s32[1]{0:T(128)} %bitcast.29.base_ref, s32[16,8]{1,0:T(8,128)} %bitcast.99, s32[2,8,2048]{2,1,0:T(8,128)} %get-tuple-element.84.slot_rows_ref, s32[2,2048,128]{2,1,0:T(8,128)} %get-tuple-element.85.slot_cols_ref, ...), custom_call_target="tpu_custom_call" | custom-call | flops 40265318400 | bytes 25165824 | tf_op jit(solution)/shard_map/pallas_call | solution.py:1228
  225.9 51.3 %shard_map.259 = (bf16[2,2048,768]{2,1,0:T(8,128)(2,1)}, bf16[2,2048,896]{2,1,0:T(8,128)(2,1)}, bf16[4,2,2,3,96,512]{5,4,3,2,1,0:T(8,128)(2,1)}) custom-call(s32[1]{0:T(128)} %bitcast.27.base_ref, s32[16,8]{1,0:T(8,128)} %bitcast.100, s32[2,8,2048]{2,1,0:T(8,128)} %get-tuple-element.84.slot_rows_ref, s32[2,2048,128]{2,1,0:T(8,128)} %get-tuple-element.85.slot_cols_ref, ...), custom_call_target="tpu_custom_call" | custom-call | flops 40265318400 | bytes 25165824 | tf_op jit(solution)/shard_map/pallas_call | solution.py:1228
  277.4 0.7 pad.23.carried_ref
  278.1 106.8 %shard_map.260 = (f32[512,768]{1,0:T(8,128)}, f32[512,128]{1,0:T(8,128)}, f32[768,256]{1,0:T(8,128)}, f32[24,896]{1,0:T(8,128)}, bf16[2048,768]{1,0:T(8,128)(2,1)}, /*index=5*/bf16[512,768]{1,0:T(8,128)(2,1)}) custom-call(f32[512,768]{1,0:T(8,128)} %get-tuple-element.76.hidden_ref, f32[512,128]{1,0:T(8,128)} %copy-done.9, bf16[512,768]{1,0:T(8,128)(2,1)} %cot_ref.3, ...), custom_call_target="tpu_custom_call" | custom-call | flops 25769803776 | bytes 25165824 | tf_op jit(solution)/shard_map/pallas_call | solution.py:791
  384.9 1.9 fusion.2
  386.8 2.2 constant_dynamic-slice_fusion
  389.0 66.3 %shard_map.261 = (f32[512,768]{1,0:T(8,128)}, f32[96,768]{1,0:T(8,128)}, f32[24,896]{1,0:T(8,128)}, bf16[2,3,96,512]{3,2,1,0:T(8,128)(2,1)}) custom-call(bf16[2048,768]{1,0:T(8,128)(2,1)} %get-tuple-element.97.grad_ref, bf16[2048,768]{1,0:T(8,128)(2,1)} %get-tuple-element.98.one_ref, bf16[768,1024]{1,0:T(8,128)(2,1)} %get-tuple-element.72.out_ref.head_ref, ...), custom_call_target="tpu_custom_call" | custom-call | flops 3221225472 | bytes 25165824 | tf_op jit(solution)/shard_map/pallas_call | solution.py:979
  455.3 0.9 fusion.5
  456.1 1.0 fusion.6
  457.2 1.4 dynamic-slice_bitcast_fusion.1
  458.6 1.3 collective-permute-start.2
  460.0 1.4 slice_reduce_fusion
  461.4 1.3 slice.127
  462.7 1.3 slice.129
  464.0 0.7 copy.79
  464.8 0.7 pad_maximum_fusion.6
  465.5 1.3 slice_bitcast_fusion.10
  466.8 1.4 slice_bitcast_fusion.1
  468.3 5.6 %collective-permute-done.2 = bf16[2,3,96,512]{3,2,1,0:T(8,128)(2,1)S(1)} collective-permute-done((bf16[2,3,96,512]{3,2,1,0:T(8,128)(2,1)S(1)}, bf16[2,3,96,512]{3,2,1,0:T(8,128)(2,1)S(1)}, u32[]{:S(2)}, u32[]{:S(2)}) %collective-permute-start.2) | collective-permute-done | bytes 589856 | tf_op jit(solution)/shard_map/ppermute | solution.py:75
  474.4 0.8 bitcast_convert_fusion
  475.2 2.0 slice.145
  477.2 1.3 slice_bitcast_fusion
  478.5 0.9 copy.84
  479.4 0.8 copy-done.12
  480.2 1.1 copy.85
  (92 shorter events, 3.2 us)
Async XLA Ops:
  7.2 9.3 %copy-start = (f32[12,12]{1,0:T(8,128)S(1)}, f32[12,12]{1,0:T(8,128)}, u32[]{:S(2)}) copy-start(f32[12,12]{1,0:T(8,128)} %param.27) | copy-start | bytes 1732
  7.2 165.0 %all-gather.7.cloned.1.call-start = ((), (), s32[]{:S(2)}) async-start(), calls=%async_computation.5 | async-start | bytes 5898240 | tf_op jit(solution)/shard_map/all_gather | solution.py:88
  7.3 2.4 copy-start.11
  10.0 4.2 copy-start.21
  10.0 4.2 copy-start.15
  10.0 4.3 copy-start.18
  10.0 4.4 copy-start.17
  10.0 4.4 copy-start.19
  11.2 20.4 %collective-permute-start = (bf16[2,3,96,512]{3,2,1,0:T(8,128)(2,1)}, bf16[2,3,96,512]{3,2,1,0:T(8,128)(2,1)S(1)}, u32[]{:S(2)}, u32[]{:S(2)}) collective-permute-start(bf16[2,3,96,512]{3,2,1,0:T(8,128)(2,1)} %get-tuple-element.189), channel_id=1, source_target_pairs={{0,4},{4,0},{8,12},{12,8},{16,20},{20,16},{24,28},{28,24},{1,5},{5... | collective-permute-start | bytes 1769480 | tf_op jit(solution)/shard_map/ppermute | solution.py:75
  14.1 13.9 %collective-permute-start.1 = (s32[2,2048]{1,0:T(2,128)S(1)}, s32[2,2048]{1,0:T(2,128)S(1)}, u32[]{:S(2)}, u32[]{:S(2)}) collective-permute-start(s32[2,2048]{1,0:T(2,128)S(1)} %bitcast.92), channel_id=1, source_target_pairs={{0,4},{4,0},{8,12},{12,8},{16,20},{20,16},{24,28},{28,24},{1,5},{5... | collective-permute-start | bytes 49160 | tf_op jit(solution)/shard_map/ppermute | solution.py:75
  14.8 1.7 copy-start.16
  14.8 2.3 copy-start.20
  14.8 2.3 copy-start.22
  16.3 1.1 copy-start.23
  17.4 70.2 %copy-start.1 = (f32[768,128]{1,0:T(8,128)}, f32[768,128]{1,0:T(8,128)S(1)}, u32[]{:S(2)}) copy-start(f32[768,128]{1,0:T(8,128)S(1)} %pad.21.mix_ref) | copy-start | bytes 1179652
  31.6 1.7 copy-start.24
  32.8 193.1 %all-gather.5.cloned.1.call-start = ((), (), s32[]{:S(2)}) async-start(), calls=%async_computation.4 | async-start | bytes 5898240 | tf_op jit(solution)/shard_map/all_gather | solution.py:88
  84.7 1.2 copy-start.25
  85.8 1.7 copy-start.4
  85.8 1.7 copy-start.5
  85.8 301.0 %reduce-scatter.3.cloned.1.call-start = ((), (), s32[]{:S(2)}) async-start(), calls=%async_computation.2 | async-start | bytes 5898240 | tf_op jit(solution)/shard_map/reduce_scatter | solution.py:92
  85.9 84.5 %copy-start.3 = (f32[1,768]{1,0:T(1,128)}, f32[1,768]{1,0:T(1,128)S(1)}, u32[]{:S(2)}) copy-start(f32[1,768]{1,0:T(1,128)S(1)} %broadcast_in_dim.21.gain_ref) | copy-start | bytes 9220
  87.5 82.9 %copy-start.2 = (s32[8,2048]{1,0:T(8,128)}, s32[8,2048]{1,0:T(8,128)S(1)}, u32[]{:S(2)}) copy-start(s32[8,2048]{1,0:T(8,128)S(1)} %copy.75.rowinfo_ref) | copy-start | bytes 196612
  87.6 1.3 copy-start.6
  88.8 1.2 copy-start.7
  170.5 1.0 copy-start.8
  171.5 0.7 copy-start.9
  172.2 53.6 %copy-start.10 = (f32[8,2048]{1,0:T(8,128)}, f32[8,2048]{1,0:T(8,128)S(1)}, u32[]{:S(2)}) copy-start(f32[8,2048]{1,0:T(8,128)S(1)} %get-tuple-element.82.total_ref) | copy-start | bytes 196612
  225.8 231.4 %reduce-scatter.5.cloned.1.call-start = ((), (), s32[]{:S(2)}) async-start(), calls=%async_computation.3 | async-start | bytes 5898240 | tf_op jit(solution)/shard_map/reduce_scatter | solution.py:92
  457.1 16.8 %copy-start.14 = (bf16[2,3,96,512]{3,2,1,0:T(8,128)(2,1)S(1)}, bf16[2,3,96,512]{3,2,1,0:T(8,128)(2,1)}, u32[]{:S(2)}) copy-start(bf16[2,3,96,512]{3,2,1,0:T(8,128)(2,1)} %get-tuple-element.108) | copy-start | bytes 1769476
  458.6 15.3 %collective-permute-start.2 = (bf16[2,3,96,512]{3,2,1,0:T(8,128)(2,1)S(1)}, bf16[2,3,96,512]{3,2,1,0:T(8,128)(2,1)S(1)}, u32[]{:S(2)}, u32[]{:S(2)}) collective-permute-start(bf16[2,3,96,512]{3,2,1,0:T(8,128)(2,1)S(1)} %get-tuple-element.187), channel_id=1, source_target_pairs={{0,4},{4,0},{8,12},{12,8},{16,20},{20,16},{24,28},{28,24},{1,5},{5... | collective-permute-start | bytes 1769480 | tf_op jit(solution)/shard_map/ppermute | solution.py:75
  477.2 1.3 copy-start.13
  478.5 1.7 copy-start.12
Sparse Core Ops, SparseCore 0:
  32.9 101.0 all-gather.6
  136.1 89.1 all-gather.4
  227.6 97.3 reduce-scatter.2
  327.2 85.7 reduce-scatter.4

commit v2 on v1

--- a/solution.py
+++ b/solution.py
@@ -158,8 +158,10 @@
             heads[c].wait_recv()
             origin = lax.rem(dp + 8 - 2 * (c + 1), 8)
             last.append(copies.start(shards.at[origin], shards.at[origin], across))
+    for move in last:
+        move.wait_recv()
     beside = [copies.start(given_ref, received_ref, across)] if columns else []
-    for move in last + near_moves + corner_moves:
+    for move in near_moves + corner_moves:
         move.wait_recv()
     if columns:
         for d in range(8):
@@ -849,12 +851,14 @@
     grad_tok_ref[...] = mine
 
     packed = refs[6] if columns else pack_ref
+    products = refs[-1]
+    products[...] = dot_tn(one_ref[...], grad_ref[...])
     along = jnp.zeros((8, width), F32)
     rest = None
     for section in range(4):
         at = slice(section * PAD, (section + 1) * PAD)
         if section < 3:
-            grad = dot_tn(one_ref[...], grad_ref[:, at])
+            grad = products[:, at]
             along = along + lax.dot_general(
                 jnp.ones((8, PAD), F32),
                 grad * head_ref[:, at].astype(F32),
@@ -889,12 +893,11 @@
         axis=1,
     )
     if columns:
-        _, pair_recv, column_send, column_recv, sums, sum_recv = refs[6:]
+        _, pair_recv, column_send, column_recv, sums, sum_recv = refs[6:-1]
         pair_moves = []
         for j in range(4):
             there = lax.rem(other(dp, 1) + 2 * j, 8)
             pair_moves.append(copies.start(packed.at[there], pair_recv.at[j], across))
-        beside = copies.start(given_ref, received_ref, across)
         sums[0] = small
         steps = [near, far, across, (other(dp, 2), lax.axis_index("tensor")), column[1]]
         sum_moves = [copies.start(sums.at[0], sum_recv.at[0], steps[0])]
@@ -921,6 +924,7 @@
                 )
             else:
                 pack_ref[...] = paired
+        beside = copies.start(given_ref, received_ref, across)
         add_up()
     else:
         sum_ref[...] = small
@@ -975,6 +979,7 @@
             pltpu.VMEM((5, *small.shape), F32),
             pltpu.VMEM((5, *small.shape), F32),
         ]
+    scratch.append(pltpu.VMEM((width, 3 * PAD), F32))
     extra = [given] if columns else []
     out = pl.pallas_call(
         functools.partial(finish_kernel, columns),
@@ -1316,10 +1321,11 @@
     cut = lambda a, g: a[g * group : (g + 1) * group]
     shards = by_parity(cut(kept, 0), swap(cut(given, 0), "dp", 1))
 
-    routes_both = jnp.stack([routes.T, swap(routes.T, "dp", 1)])
-    slot_rows, slot_cols, info = route(routes_both)
+    angles, routes_there = together(
+        rotary_angles(segment_ids, parent_ids), swap(routes.T, "dp", 1)
+    )
+    slot_rows, slot_cols, info = route(jnp.stack([routes.T, routes_there]))
     info = info.reshape(2 * NF, -1)[:, :8]
-    angles = rotary_angles(segment_ids, parent_ids)
     rowinfo = jnp.pad(jnp.stack([segment_ids, parent_ids]), ((0, 6), (0, 0)))
     colinfo = rowinfo.T
     local_routes = lax.dynamic_slice_in_dim(routes, index * row_count, row_count, 0)

time: 495 us -> 482 us (0.974)
  Pallas kernels: 406 us -> 396 us
  waiting for transfers between devices: 14.9 us -> 8.53 us
    pallas_call x1, Pallas kernels: 66.3 us -> 54.7 us  [finish(): pl.pallas_call(functools.partial(finish_kernel, columns), in_specs=[vmem]...]
    ppermute x3, waiting for transfers between devices: 14.8 us -> 8.43 us  [swap(): return lax.ppermute(values, axis, [(i, i ^ bits) for i in range(size)])]
    pallas_call x2, Pallas kernels: 105 us -> 111 us  [experts(): pl.pallas_call(functools.partial(experts_kernel, whole_weights, len(befor...]
  transfers between devices with their start and end apart: 7 -> 7, of which waited for: 2 -> 2; matrix products, arithmetic and copies ran while one was open for 6% -> 6% of each run, Pallas kernels for 83% -> 84%
where the time goes in v2:
time: 482 us; the launch traced here: 473 us
  Pallas kernels  396 us (82%)
  local copies, waits for them, and re-layouts  31.8 us (7%)
  between operations  14.6 us (3%)
  other arithmetic  14.4 us (3%)
  waiting for transfers between devices  8.53 us (2%)
  starting transfers between devices  5.11 us (1%)
    pallas_call x2, Pallas kernels, experts(): pl.pallas_call(functools.partial(experts_kernel, whole_weights, len(befor...  111 us
    pallas_call x1, Pallas kernels, branch_back(): pl.pallas_call(functools.partial(branch_back_kernel, heads), in_specs=[vm...  102 us
    pallas_call x1, Pallas kernels, branch(): pl.pallas_call(functools.partial(branch_kernel, heads), in_specs=[vmem] *...  80.7 us
    pallas_call x1, Pallas kernels, finish(): pl.pallas_call(functools.partial(finish_kernel, columns), in_specs=[vmem]...  54.7 us
    pallas_call x1, Pallas kernels, project(): pl.pallas_call(functools.partial(project_kernel, columns), in_specs=[vmem...  44.2 us
  transfers between devices with their start and end apart: 7, of which 2 were waited for; matrix products, arithmetic and copies ran while one was open for 6% of the time, Pallas kernels for 84%

profile of v2, /device:TPU:0, one launch (start us, length us, event | category | flops | bytes accessed | tf_op | source)
XLA Modules:
  0.0 472.9 jit_solution(12710927532322714985)
XLA Ops:
  7.3 2.2 convert_element_type.32
  10.0 1.1 fusion.4
  11.2 3.0 collective-permute-start.1
  15.5 1.5 pad_bitcast_fusion
  17.0 3.7 multiply_cosine_fusion
  20.7 0.6 fusion.7
  21.3 1.3 pad_maximum_fusion.5.angle_ref
  23.4 0.6 pad.22.vector_ref
  24.0 0.8 concatenate.67.pack_ref
  24.7 3.3 collective-permute-done
  28.0 0.6 pad_add_fusion.routes_ref
  28.6 2.9 shard_map.255
  31.6 1.1 pad_maximum_fusion.1
  33.3 0.6 broadcast_in_dim.17.gain_ref
  33.9 44.2 %shard_map.256 = (bf16[2048,256]{1,0:T(8,128)(2,1)}, bf16[2048,256]{1,0:T(8,128)(2,1)}, bf16[2048,256]{1,0:T(8,128)(2,1)}, bf16[256,2048]{1,0:T(8,128)(2,1)}, bf...) custom-call(bf16[512,768]{1,0:T(8,128)(2,1)} %tok_ref.5, ...), custom_call_target="tpu_custom_call" | custom-call | flops 2415919104 | bytes 25165824 | tf_op jit(solution)/shard_map/pallas_call | solution.py:218
  78.0 1.2 select_bitcast_fusion.1
  79.2 1.1 pad_maximum_fusion.2
  80.4 1.6 copy.75.rowinfo_ref
  82.1 1.3 copy-done.6
  83.4 1.2 copy-done.7
  84.6 80.7 %shard_map.257 = (bf16[2048,256]{1,0:T(8,128)(2,1)S(1)}, f32[8,2048]{1,0:T(8,128)S(1)}, f32[512,768]{1,0:T(8,128)}, f32[512,128]{1,0:T(8,128)S(1)}, bf16[2,2048,...) custom-call(bf16[2048,256]{1,0:T(8,128)(2,1)S(1)} %copy-done.6, bf16[2048,256]{1,0:T(8,128)(2,1)S(1)} %copy-done.7, ...), custom_call_target="tpu_custom_call" | custom-call | flops 6442450944 | bytes 25165824 | tf_op jit(solution)/shard_map/pallas_call | solution.py:475
  165.3 1.0 copy-done.8
  166.3 0.7 copy-done.9
  167.0 53.6 %shard_map.258 = (bf16[2,2048,768]{2,1,0:T(8,128)(2,1)}, bf16[2,2048,896]{2,1,0:T(8,128)(2,1)}, bf16[4,2,2,3,96,512]{5,4,3,2,1,0:T(8,128)(2,1)}) custom-call(s32[1]{0:T(128)} %bitcast.29.base_ref, s32[16,8]{1,0:T(8,128)} %bitcast.99, s32[2,8,2048]{2,1,0:T(8,128)} %get-tuple-element.88.slot_rows_ref, s32[2,2048,128]{2,1,0:T(8,128)} %get-tuple-element.89.slot_cols_ref, ...), custom_call_target="tpu_custom_call" | custom-call | flops 40265318400 | bytes 25165824 | tf_op jit(solution)/shard_map/pallas_call | solution.py:1233
  220.8 57.5 %shard_map.259 = (bf16[2,2048,768]{2,1,0:T(8,128)(2,1)}, bf16[2,2048,896]{2,1,0:T(8,128)(2,1)}, bf16[4,2,2,3,96,512]{5,4,3,2,1,0:T(8,128)(2,1)}) custom-call(s32[1]{0:T(128)} %bitcast.27.base_ref, s32[16,8]{1,0:T(8,128)} %bitcast.100, s32[2,8,2048]{2,1,0:T(8,128)} %get-tuple-element.88.slot_rows_ref, s32[2,2048,128]{2,1,0:T(8,128)} %get-tuple-element.89.slot_cols_ref, ...), custom_call_target="tpu_custom_call" | custom-call | flops 40265318400 | bytes 25165824 | tf_op jit(solution)/shard_map/pallas_call | solution.py:1233
  278.5 0.7 pad.23.carried_ref
  279.2 102.4 %shard_map.260 = (f32[512,768]{1,0:T(8,128)}, f32[512,128]{1,0:T(8,128)}, f32[768,256]{1,0:T(8,128)}, f32[24,896]{1,0:T(8,128)}, bf16[2048,768]{1,0:T(8,128)(2,1)}, /*index=5*/bf16[512,768]{1,0:T(8,128)(2,1)}) custom-call(f32[512,768]{1,0:T(8,128)} %get-tuple-element.80.hidden_ref, f32[512,128]{1,0:T(8,128)} %copy-done.9, bf16[512,768]{1,0:T(8,128)(2,1)} %cot_ref.3, ...), custom_call_target="tpu_custom_call" | custom-call | flops 25769803776 | bytes 25165824 | tf_op jit(solution)/shard_map/pallas_call | solution.py:793
  381.6 1.9 fusion.2
  383.6 2.2 constant_dynamic-slice_fusion
  385.8 54.7 %shard_map.261 = (f32[512,768]{1,0:T(8,128)}, f32[96,768]{1,0:T(8,128)}, f32[24,896]{1,0:T(8,128)}, bf16[2,3,96,512]{3,2,1,0:T(8,128)(2,1)}) custom-call(bf16[2048,768]{1,0:T(8,128)(2,1)} %get-tuple-element.101.grad_ref, bf16[2048,768]{1,0:T(8,128)(2,1)} %get-tuple-element.102.one_ref, bf16[768,1024]{1,0:T(8,128)(2,1)} %get-tuple-element.76.out_ref.head_ref, ...), custom_call_target="tpu_custom_call" | custom-call | flops 3221225472 | bytes 25165824 | tf_op jit(solution)/shard_map/pallas_call | solution.py:984
  440.4 0.9 fusion.5
  441.3 1.0 fusion.6
  442.3 1.4 dynamic-slice_bitcast_fusion.1
  443.8 1.5 collective-permute-start.2
  445.3 1.4 slice_reduce_fusion
  446.8 1.3 slice.127
  448.1 1.3 slice.129
  449.4 0.7 copy.79
  450.1 0.7 pad_maximum_fusion.6
  450.9 1.3 slice_bitcast_fusion.10
  452.2 1.4 slice_bitcast_fusion.1
  453.6 5.2 %collective-permute-done.2 = bf16[2,3,96,512]{3,2,1,0:T(8,128)(2,1)S(1)} collective-permute-done((bf16[2,3,96,512]{3,2,1,0:T(8,128)(2,1)S(1)}, bf16[2,3,96,512]{3,2,1,0:T(8,128)(2,1)S(1)}, u32[]{:S(2)}, u32[]{:S(2)}) %collective-permute-start.2) | collective-permute-done | bytes 589856 | tf_op jit(solution)/shard_map/ppermute | solution.py:75
  459.2 0.8 bitcast_convert_fusion
  460.0 2.0 slice.145
  462.1 1.3 slice_bitcast_fusion
  463.4 0.9 copy.84
  464.3 0.8 copy-done.12
  465.1 1.1 copy.85
  (92 shorter events, 3.9 us)
Async XLA Ops:
  7.2 13.5 %copy-start = (f32[12,12]{1,0:T(8,128)S(1)}, f32[12,12]{1,0:T(8,128)}, u32[]{:S(2)}) copy-start(f32[12,12]{1,0:T(8,128)} %param.27) | copy-start | bytes 1732
  7.2 159.8 %all-gather.7.cloned.1.call-start = ((), (), s32[]{:S(2)}) async-start(), calls=%async_computation.5 | async-start | bytes 5898240 | tf_op jit(solution)/shard_map/all_gather | solution.py:88
  7.3 2.4 copy-start.11
  10.0 4.2 copy-start.21
  10.0 4.2 copy-start.15
  10.0 4.3 copy-start.18
  10.0 4.4 copy-start.17
  10.0 4.9 %copy-start.19 = (s32[2048]{0:T(1024)S(1)}, s32[2048]{0:T(1024)}, u32[]{:S(2)}) copy-start(s32[2048]{0:T(1024)} %param.20) | copy-start | bytes 24580
  11.2 20.4 %collective-permute-start.1 = (bf16[2,3,96,512]{3,2,1,0:T(8,128)(2,1)}, bf16[2,3,96,512]{3,2,1,0:T(8,128)(2,1)S(1)}, u32[]{:S(2)}, u32[]{:S(2)}) collective-permute-start(bf16[2,3,96,512]{3,2,1,0:T(8,128)(2,1)} %get-tuple-element.193), channel_id=1, source_target_pairs={{0,4},{4,0},{8,12},{12,8},{16,20},{20,16},{24,28},{28,24},{1,5},{5... | collective-permute-start | bytes 1769480 | tf_op jit(solution)/shard_map/ppermute | solution.py:75
  14.1 13.9 %collective-permute-start = (s32[2,2048]{1,0:T(2,128)S(1)}, s32[2,2048]{1,0:T(2,128)S(1)}, u32[]{:S(2)}, u32[]{:S(2)}) collective-permute-start(s32[2,2048]{1,0:T(2,128)S(1)} %bitcast.92), channel_id=1, source_target_pairs={{0,4},{4,0},{8,12},{12,8},{16,20},{20,16},{24,28},{28,24},{1,5},{5... | collective-permute-start | bytes 49160 | tf_op jit(solution)/shard_map/ppermute | solution.py:75
  16.9 3.8 copy-start.16
  21.3 1.4 copy-start.20
  21.3 1.4 copy-start.22
  22.7 0.7 copy-start.23
  22.9 59.2 %copy-start.1 = (f32[768,128]{1,0:T(8,128)}, f32[768,128]{1,0:T(8,128)S(1)}, u32[]{:S(2)}) copy-start(f32[768,128]{1,0:T(8,128)S(1)} %pad.21.mix_ref) | copy-start | bytes 1179652
  31.6 1.7 copy-start.24
  32.8 188.0 %all-gather.5.cloned.1.call-start = ((), (), s32[]{:S(2)}) async-start(), calls=%async_computation.4 | async-start | bytes 5898240 | tf_op jit(solution)/shard_map/all_gather | solution.py:88
  79.2 1.2 copy-start.25
  80.3 1.7 copy-start.4
  80.3 1.7 copy-start.5
  80.4 303.2 %reduce-scatter.3.cloned.1.call-start = ((), (), s32[]{:S(2)}) async-start(), calls=%async_computation.2 | async-start | bytes 5898240 | tf_op jit(solution)/shard_map/reduce_scatter | solution.py:92
  80.4 84.9 %copy-start.3 = (f32[1,768]{1,0:T(1,128)}, f32[1,768]{1,0:T(1,128)S(1)}, u32[]{:S(2)}) copy-start(f32[1,768]{1,0:T(1,128)S(1)} %broadcast_in_dim.21.gain_ref) | copy-start | bytes 9220
  82.1 83.3 %copy-start.2 = (s32[8,2048]{1,0:T(8,128)}, s32[8,2048]{1,0:T(8,128)S(1)}, u32[]{:S(2)}) copy-start(s32[8,2048]{1,0:T(8,128)S(1)} %copy.75.rowinfo_ref) | copy-start | bytes 196612
  82.1 1.3 copy-start.6
  83.3 1.2 copy-start.7
  165.3 1.0 copy-start.8
  166.3 0.7 copy-start.9
  167.0 53.6 %copy-start.10 = (f32[8,2048]{1,0:T(8,128)}, f32[8,2048]{1,0:T(8,128)S(1)}, u32[]{:S(2)}) copy-start(f32[8,2048]{1,0:T(8,128)S(1)} %get-tuple-element.86.total_ref) | copy-start | bytes 196612
  220.7 221.7 %reduce-scatter.5.cloned.1.call-start = ((), (), s32[]{:S(2)}) async-start(), calls=%async_computation.3 | async-start | bytes 5898240 | tf_op jit(solution)/shard_map/reduce_scatter | solution.py:92
  442.3 16.5 %copy-start.14 = (bf16[2,3,96,512]{3,2,1,0:T(8,128)(2,1)S(1)}, bf16[2,3,96,512]{3,2,1,0:T(8,128)(2,1)}, u32[]{:S(2)}) copy-start(bf16[2,3,96,512]{3,2,1,0:T(8,128)(2,1)} %get-tuple-element.112) | copy-start | bytes 1769476
  443.8 15.0 %collective-permute-start.2 = (bf16[2,3,96,512]{3,2,1,0:T(8,128)(2,1)S(1)}, bf16[2,3,96,512]{3,2,1,0:T(8,128)(2,1)S(1)}, u32[]{:S(2)}, u32[]{:S(2)}) collective-permute-start(bf16[2,3,96,512]{3,2,1,0:T(8,128)(2,1)S(1)} %get-tuple-element.191), channel_id=1, source_target_pairs={{0,4},{4,0},{8,12},{12,8},{16,20},{20,16},{24,28},{28,24},{1,5},{5... | collective-permute-start | bytes 1769480 | tf_op jit(solution)/shard_map/ppermute | solution.py:75
  462.1 1.3 copy-start.13
  463.4 1.7 copy-start.12
Sparse Core Ops, SparseCore 0:
  32.9 95.8 all-gather.6
  130.9 89.2 all-gather.4
  222.5 92.5 reduce-scatter.2
  317.2 85.7 reduce-scatter.4

commit v3 on v2

--- a/solution.py
+++ b/solution.py
@@ -924,7 +924,7 @@
                 )
             else:
                 pack_ref[...] = paired
-        beside = copies.start(given_ref, received_ref, across)
+        beside = copies.start(given_ref.at[1 - lax.rem(dp, 2)], received_ref, across)
         add_up()
     else:
         sum_ref[...] = small
@@ -990,7 +990,7 @@
             pack,
             jax.ShapeDtypeStruct(small.shape, F32),
         ]
-        + [jax.ShapeDtypeStruct(a.shape, a.dtype) for a in extra],
+        + [jax.ShapeDtypeStruct(a.shape[1:], a.dtype) for a in extra],
         scratch_shapes=scratch,
         compiler_params=pltpu.CompilerParams(
             collective_id=4, has_side_effects=True, vmem_limit_bytes=56 << 20
@@ -999,7 +999,10 @@
             flops=32 * rows * width * PAD, bytes_accessed=64 * rows * width, transcendentals=0
         ),
     )(grads, ones, head_full, grad_out, small, grad_hidden, tokens, gain[None], *extra)
-    return out if columns else [*out, swap(given, "dp", 1)]
+    if columns:
+        return out
+    there = 1 - lax.axis_index("dp") % 2
+    return [*out, swap(lax.dynamic_index_in_dim(given, there, 0, keepdims=False), "dp", 1)]
 
 
 def route_kernel(routes_ref, rows_ref, cols_ref, info_ref):
@@ -1373,15 +1376,16 @@
         attended, head_full, queries, keys, values, keys_t, rowinfo, colinfo, totals, angles, sums,
         grad_ins,
     )
-    grad_carried = lax.dot_general(
-        grad_logits[:, :NE], carry_weight, (((1,), (1,)), ((), ())), precision=HIGHEST
-    )
     mine = lambda a: lax.dynamic_index_in_dim(a, parity, 0, keepdims=False)
     theirs = lambda a: lax.dynamic_index_in_dim(a, 1 - parity, 0, keepdims=False)
     grad_projected, own_grads[0] = together(grad_projected, own_grads[0])
     grad_tokens, own_pack, small, received = finish(
         columns, grad_projected, gathered_one, head_full, grad_output_t, small, grad_hidden, tokens_in,
-        attention_gain, theirs(own_grads[0]),
+        attention_gain, own_grads[0],
+    )
+    grad_logits, own_pack = together(grad_logits, own_pack)
+    grad_carried = lax.dot_general(
+        grad_logits[:, :NE], carry_weight, (((1,), (1,)), ((), ())), precision=HIGHEST
     )
     if columns:
         own_sections = [

time: 482 us -> 483 us (level); the launches traced: 473 us -> 480 us
  Pallas kernels: 396 us -> 405 us
    pallas_call x1, Pallas kernels: 54.7 us -> 62.8 us  [finish(): pl.pallas_call(functools.partial(finish_kernel, columns), in_specs=[vmem]...]
    pallas_call x1, Pallas kernels: 102 us -> 108 us  [branch_back(): pl.pallas_call(functools.partial(branch_back_kernel, heads), in_specs=[vm...]
where the time goes in v3:
time: 483 us; the launch traced here: 480 us
  Pallas kernels  405 us (84%)
  local copies, waits for them, and re-layouts  31.9 us (7%)
  other arithmetic  15 us (3%)
  between operations  14.6 us (3%)
  waiting for transfers between devices  6.75 us (1%)
    pallas_call x1, Pallas kernels, branch_back(): pl.pallas_call(functools.partial(branch_back_kernel, heads), in_specs=[vm...  108 us
    pallas_call x2, Pallas kernels, experts(): pl.pallas_call(functools.partial(experts_kernel, whole_weights, len(befor...  107 us
    pallas_call x1, Pallas kernels, branch(): pl.pallas_call(functools.partial(branch_kernel, heads), in_specs=[vmem] *...  80.7 us
    pallas_call x1, Pallas kernels, finish(): pl.pallas_call(functools.partial(finish_kernel, columns), in_specs=[vmem]...  62.8 us
    pallas_call x1, Pallas kernels, project(): pl.pallas_call(functools.partial(project_kernel, columns), in_specs=[vmem...  44.2 us
  transfers between devices with their start and end apart: 7, of which 2 were waited for; matrix products, arithmetic and copies ran while one was open for 6% of the time, Pallas kernels for 84%

profile of v3, /device:TPU:0, one launch (start us, length us, event | category | flops | bytes accessed | tf_op | source)
XLA Modules:
  0.0 479.9 jit_solution(5749501374831094911)
XLA Ops:
  7.3 2.2 convert_element_type.32
  10.0 1.1 fusion.4
  11.2 3.0 collective-permute-start.1
  15.5 1.5 pad_bitcast_fusion
  17.0 3.7 multiply_cosine_fusion
  20.7 0.6 fusion.7
  21.3 1.3 pad_maximum_fusion.5.angle_ref
  23.3 0.6 pad.22.vector_ref
  24.0 0.8 concatenate.67.pack_ref
  24.7 3.3 collective-permute-done
  28.0 0.6 pad_add_fusion.routes_ref
  28.6 2.9 shard_map.255
  31.6 1.1 pad_maximum_fusion.1
  32.8 0.5 all-gather.5.cloned.1.call-start
  33.3 0.6 broadcast_in_dim.17.gain_ref
  33.9 44.2 %shard_map.256 = (bf16[2048,256]{1,0:T(8,128)(2,1)}, bf16[2048,256]{1,0:T(8,128)(2,1)}, bf16[2048,256]{1,0:T(8,128)(2,1)}, bf16[256,2048]{1,0:T(8,128)(2,1)}, bf...) custom-call(bf16[512,768]{1,0:T(8,128)(2,1)} %tok_ref.5, ...), custom_call_target="tpu_custom_call" | custom-call | flops 2415919104 | bytes 25165824 | tf_op jit(solution)/shard_map/pallas_call | solution.py:218
  78.1 1.2 select_bitcast_fusion.1
  79.2 1.1 pad_maximum_fusion.2
  80.5 1.6 copy.75.rowinfo_ref
  82.1 1.3 copy-done.6
  83.4 1.2 copy-done.7
  84.6 80.7 %shard_map.257 = (bf16[2048,256]{1,0:T(8,128)(2,1)S(1)}, f32[8,2048]{1,0:T(8,128)S(1)}, f32[512,768]{1,0:T(8,128)}, f32[512,128]{1,0:T(8,128)S(1)}, bf16[2,2048,...) custom-call(bf16[2048,256]{1,0:T(8,128)(2,1)S(1)} %copy-done.6, bf16[2048,256]{1,0:T(8,128)(2,1)S(1)} %copy-done.7, ...), custom_call_target="tpu_custom_call" | custom-call | flops 6442450944 | bytes 25165824 | tf_op jit(solution)/shard_map/pallas_call | solution.py:475
  165.3 1.0 copy-done.8
  166.3 0.7 copy-done.9
  167.0 55.2 %shard_map.258 = (bf16[2,2048,768]{2,1,0:T(8,128)(2,1)}, bf16[2,2048,896]{2,1,0:T(8,128)(2,1)}, bf16[4,2,2,3,96,512]{5,4,3,2,1,0:T(8,128)(2,1)}) custom-call(s32[1]{0:T(128)} %bitcast.29.base_ref, s32[16,8]{1,0:T(8,128)} %bitcast.98, s32[2,8,2048]{2,1,0:T(8,128)} %get-tuple-element.90.slot_rows_ref, s32[2,2048,128]{2,1,0:T(8,128)} %get-tuple-element.91.slot_cols_ref, ...), custom_call_target="tpu_custom_call" | custom-call | flops 40265318400 | bytes 25165824 | tf_op jit(solution)/shard_map/pallas_call | solution.py:1236
  222.3 51.3 %shard_map.259 = (bf16[2,2048,768]{2,1,0:T(8,128)(2,1)}, bf16[2,2048,896]{2,1,0:T(8,128)(2,1)}, bf16[4,2,2,3,96,512]{5,4,3,2,1,0:T(8,128)(2,1)}) custom-call(s32[1]{0:T(128)} %bitcast.27.base_ref, s32[16,8]{1,0:T(8,128)} %bitcast.99, s32[2,8,2048]{2,1,0:T(8,128)} %get-tuple-element.90.slot_rows_ref, s32[2,2048,128]{2,1,0:T(8,128)} %get-tuple-element.91.slot_cols_ref, ...), custom_call_target="tpu_custom_call" | custom-call | flops 40265318400 | bytes 25165824 | tf_op jit(solution)/shard_map/pallas_call | solution.py:1236
  273.9 0.7 pad.23.carried_ref
  274.6 108.2 %shard_map.260 = (f32[512,768]{1,0:T(8,128)}, f32[512,128]{1,0:T(8,128)}, f32[768,256]{1,0:T(8,128)}, f32[24,896]{1,0:T(8,128)}, bf16[2048,768]{1,0:T(8,128)(2,1)}, /*index=5*/bf16[512,768]{1,0:T(8,128)(2,1)}) custom-call(f32[512,768]{1,0:T(8,128)} %get-tuple-element.82.hidden_ref, f32[512,128]{1,0:T(8,128)} %copy-done.9, bf16[512,768]{1,0:T(8,128)(2,1)} %cot_ref.3, ...), custom_call_target="tpu_custom_call" | custom-call | flops 25769803776 | bytes 25165824 | tf_op jit(solution)/shard_map/pallas_call | solution.py:793
  382.8 62.8 %shard_map.261 = (f32[512,768]{1,0:T(8,128)}, f32[96,768]{1,0:T(8,128)}, f32[24,896]{1,0:T(8,128)}, bf16[2,3,96,512]{3,2,1,0:T(8,128)(2,1)}) custom-call(bf16[2048,768]{1,0:T(8,128)(2,1)} %get-tuple-element.103.grad_ref, bf16[2048,768]{1,0:T(8,128)(2,1)} %get-tuple-element.104.one_ref, bf16[768,1024]{1,0:T(8,128)(2,1)} %get-tuple-element.78.out_ref.head_ref, ...), custom_call_target="tpu_custom_call" | custom-call | flops 3221225472 | bytes 25165824 | tf_op jit(solution)/shard_map/pallas_call | solution.py:984
  445.6 1.5 fusion.5
  447.2 1.6 fusion.6
  448.9 1.5 dynamic-slice_bitcast_fusion.1
  450.5 1.3 slice_bitcast_fusion.10
  451.8 0.6 maximum_bitcast_fusion.3
  452.5 0.7 pad_maximum_fusion.6
  453.3 1.4 slice_reduce_fusion
  454.7 1.3 slice.127
  456.0 1.3 slice.129
  457.3 1.6 copy.79
  459.0 1.4 slice_bitcast_fusion.1
  460.4 1.9 fusion.2
  462.4 3.4 collective-permute-done.2
  466.2 0.8 bitcast_convert_fusion
  467.0 2.0 slice.145
  469.0 1.3 slice_bitcast_fusion
  470.3 0.9 copy.84
  471.2 0.8 copy-done.13
  472.0 1.1 copy.85
  (110 shorter events, 3.6 us)
Async XLA Ops:
  7.2 13.5 %copy-start = (f32[12,12]{1,0:T(8,128)S(1)}, f32[12,12]{1,0:T(8,128)}, u32[]{:S(2)}) copy-start(f32[12,12]{1,0:T(8,128)} %param.27) | copy-start | bytes 1732
  7.2 159.8 %all-gather.7.cloned.1.call-start = ((), (), s32[]{:S(2)}) async-start(), calls=%async_computation.5 | async-start | bytes 5898240 | tf_op jit(solution)/shard_map/all_gather | solution.py:88
  7.3 2.4 copy-start.12
  10.0 4.2 copy-start.30
  10.0 4.2 copy-start.16
  10.0 4.3 copy-start.27
  10.0 4.4 copy-start.26
  10.0 4.9 %copy-start.28 = (s32[2048]{0:T(1024)S(1)}, s32[2048]{0:T(1024)}, u32[]{:S(2)}) copy-start(s32[2048]{0:T(1024)} %param.20) | copy-start | bytes 24580
  11.2 20.4 %collective-permute-start.1 = (bf16[2,3,96,512]{3,2,1,0:T(8,128)(2,1)}, bf16[2,3,96,512]{3,2,1,0:T(8,128)(2,1)S(1)}, u32[]{:S(2)}, u32[]{:S(2)}) collective-permute-start(bf16[2,3,96,512]{3,2,1,0:T(8,128)(2,1)} %get-tuple-element.195), channel_id=1, source_target_pairs={{0,4},{4,0},{8,12},{12,8},{16,20},{20,16},{24,28},{28,24},{1,5},{5... | collective-permute-start | bytes 1769480 | tf_op jit(solution)/shard_map/ppermute | solution.py:75
  14.1 13.9 %collective-permute-start = (s32[2,2048]{1,0:T(2,128)S(1)}, s32[2,2048]{1,0:T(2,128)S(1)}, u32[]{:S(2)}, u32[]{:S(2)}) collective-permute-start(s32[2,2048]{1,0:T(2,128)S(1)} %bitcast.91), channel_id=1, source_target_pairs={{0,4},{4,0},{8,12},{12,8},{16,20},{20,16},{24,28},{28,24},{1,5},{5... | collective-permute-start | bytes 49160 | tf_op jit(solution)/shard_map/ppermute | solution.py:75
  16.9 3.8 copy-start.25
  21.3 1.4 copy-start.29
  21.3 1.3 copy-start.31
  22.7 0.7 copy-start.32
  22.9 59.2 %copy-start.2 = (f32[768,128]{1,0:T(8,128)}, f32[768,128]{1,0:T(8,128)S(1)}, u32[]{:S(2)}) copy-start(f32[768,128]{1,0:T(8,128)S(1)} %pad.21.mix_ref) | copy-start | bytes 1179652
  31.6 1.7 copy-start.33
  32.8 189.6 %all-gather.5.cloned.1.call-start = ((), (), s32[]{:S(2)}) async-start(), calls=%async_computation.4 | async-start | bytes 5898240 | tf_op jit(solution)/shard_map/all_gather | solution.py:88
  79.2 1.2 copy-start.34
  80.3 1.7 copy-start.1
  80.4 1.7 copy-start.5
  80.4 302.5 %reduce-scatter.3.cloned.1.call-start = ((), (), s32[]{:S(2)}) async-start(), calls=%async_computation.2 | async-start | bytes 5898240 | tf_op jit(solution)/shard_map/reduce_scatter | solution.py:92
  80.4 84.9 %copy-start.4 = (f32[1,768]{1,0:T(1,128)}, f32[1,768]{1,0:T(1,128)S(1)}, u32[]{:S(2)}) copy-start(f32[1,768]{1,0:T(1,128)S(1)} %broadcast_in_dim.21.gain_ref) | copy-start | bytes 9220
  82.1 83.2 %copy-start.3 = (s32[8,2048]{1,0:T(8,128)}, s32[8,2048]{1,0:T(8,128)S(1)}, u32[]{:S(2)}) copy-start(s32[8,2048]{1,0:T(8,128)S(1)} %copy.75.rowinfo_ref) | copy-start | bytes 196612
  82.1 1.3 copy-start.6
  83.4 1.2 copy-start.7
  165.3 1.0 copy-start.8
  166.3 0.7 copy-start.9
  167.0 55.2 %copy-start.10 = (f32[8,2048]{1,0:T(8,128)}, f32[8,2048]{1,0:T(8,128)S(1)}, u32[]{:S(2)}) copy-start(f32[8,2048]{1,0:T(8,128)S(1)} %get-tuple-element.88.total_ref) | copy-start | bytes 196612
  222.3 226.5 %reduce-scatter.5.cloned.1.call-start = ((), (), s32[]{:S(2)}) async-start(), calls=%async_computation.3 | async-start | bytes 5898240 | tf_op jit(solution)/shard_map/reduce_scatter | solution.py:92
  448.8 10.2 %copy-start.11 = (bf16[1,2,2,3,96,512]{5,4,3,2,1,0:T(8,128)(2,1)S(1)}, bf16[1,2,2,3,96,512]{5,4,3,2,1,0:T(8,128)(2,1)}, u32[]{:S(2)}) copy-start(bf16[1,2,2,3,96,512]{5,4,3,2,1,0:T(8,128)(2,1)} %reduce-scatter.3.cloned.1.call-done) | copy-start | bytes 3538948
  448.8 3.0 copy-start.21
  448.8 3.0 copy-start.24
  448.8 3.6 copy-start.20
  448.8 3.6 copy-start.23
  448.9 3.6 copy-start.18
  448.9 3.6 copy-start.22
  448.9 3.6 copy-start.17
  448.9 3.6 copy-start.19
  450.4 15.3 %collective-permute-start.2 = (bf16[2,3,96,512]{3,2,1,0:T(8,128)(2,1)S(1)}, bf16[2,3,96,512]{3,2,1,0:T(8,128)(2,1)S(1)}, u32[]{:S(2)}, u32[]{:S(2)}) collective-permute-start(bf16[2,3,96,512]{3,2,1,0:T(8,128)(2,1)S(1)} %get-tuple-element.193), channel_id=1, source_target_pairs={{0,4},{4,0},{8,12},{12,8},{16,20},{20,16},{24,28},{28,24},{1,5},{5... | collective-permute-start | bytes 1769480 | tf_op jit(solution)/shard_map/ppermute | solution.py:75
  451.8 13.9 %copy-start.15 = (bf16[2,3,96,512]{3,2,1,0:T(8,128)(2,1)S(1)}, bf16[2,3,96,512]{3,2,1,0:T(8,128)(2,1)}, u32[]{:S(2)}) copy-start(bf16[2,3,96,512]{3,2,1,0:T(8,128)(2,1)} %get-tuple-element.116) | copy-start | bytes 1769476
  469.0 1.3 copy-start.14
  470.3 1.7 copy-start.13
Sparse Core Ops, SparseCore 0:
  32.9 95.8 all-gather.6
  130.9 89.2 all-gather.4
  222.5 94.5 reduce-scatter.2
  319.3 85.7 reduce-scatter.4
